TPU v7x, 256 devices: a whole 4x4x8 slice. The times are simulated.
256 devices in a mesh: expert: 32 (over z, y), dp: 8 (over x, core).
Axes of the slice: x: 4, y: 4, z: 8, core: 2. Of those that a mesh axis runs over, the one named last changes fastest.
Arguments:
- tokens: bfloat16 [8192, 2048], P(('dp', 'expert')), may hold values from -6 to 6
- expert_ids: int32 [8192, 2], P(('dp', 'expert')), may hold values from 0 to 31, all different within a row; in each aligned block of 32 rows (0 to 31, 32 to 63, ...) at most 4 rows name the same one
- gates: float32 [8192, 2], P(('dp', 'expert')), may hold values from 0.1 to 1
- valid: int32 [8192], P(('dp', 'expert')), may hold values 0 or 1
- w_in: bfloat16 [32, 2048, 8192], P('expert', None, 'dp'), may hold values from -0.125 to 0.125
- w_out: bfloat16 [32, 8192, 2048], P('expert', 'dp'), may hold values from -0.0625 to 0.0625
- up_proj: bfloat16 [2048, 8192], P(None, 'expert'), may hold values from -0.125 to 0.125
- down_proj: bfloat16 [8192, 2048], P('expert'), may hold values from -0.0625 to 0.0625
Outputs:
- grad_up: float32 [2048, 8192], P('dp', 'expert')
- grad_down: float32 [8192, 2048], P('expert', 'dp')
Inputs may be any that keep to these rules, and one draw needn't show every extreme that they name: `expert_ids`: the two experts of a token differ; among the 32 rows of one device no expert is named more than 4 times, a bound that some block reaches.
All inputs are finite; a program needn't handle non-finite values. No bound on the sum of `valid` on one device may be relied on, other than what follows from the above.
Results may differ from a plain program's by a relative error of at most 0.017.
Values may be sent and summed in bfloat16 or wider, within the bound.
A program may use at most 64 MiB of HBM per device.

v0:
```python
import jax
import jax.numpy as jnp
from jax import lax
from jax.sharding import PartitionSpec as P


def silu_grad(preact):
    sigmoid = jax.nn.sigmoid(preact)
    return sigmoid * (1.0 + preact * (1.0 - sigmoid))


def per_device(tokens, expert_ids, gates, valid, w_in, w_out, up_proj, down_proj):
    n_expert = lax.axis_size("expert")
    n_data = lax.axis_size("dp")
    tok_count = tokens.shape[0]
    capacity = 4 * tok_count // n_expert
    slot_width = n_expert * capacity
    flat_ids = expert_ids.reshape(-1)
    expert_hot = (flat_ids[:, None] == jnp.arange(n_expert, dtype=jnp.int32)[None, :]).astype(
        jnp.int32
    )
    ranks = jnp.sum((jnp.cumsum(expert_hot, axis=0) - 1) * expert_hot, axis=1)
    slots = flat_ids * capacity + ranks
    slot_hot = (slots[:, None] == jnp.arange(slot_width, dtype=jnp.int32)[None, :]).astype(
        jnp.bfloat16
    )
    paired = slot_hot.reshape(tok_count, 2, slot_width)
    placing = paired[:, 0, :] + paired[:, 1, :]
    outgoing = lax.dot_general(
        placing, tokens, (((0,), (0,)), ((), ())), preferred_element_type=jnp.float32
    ).astype(jnp.bfloat16)
    stacked = lax.all_gather(
        outgoing.reshape(1, n_expert, capacity, tokens.shape[1]), "dp", axis=0, tiled=True
    )
    arrived = lax.all_to_all(stacked, "expert", split_axis=1, concat_axis=2, tiled=True)
    expert_rows = arrived.reshape(n_data * slot_width, tokens.shape[1])
    inner_weight = w_in[0]
    outer_weight = w_out[0]
    teacher_hidden = jax.nn.relu(
        jnp.dot(expert_rows, inner_weight, preferred_element_type=jnp.float32)
    ).astype(jnp.bfloat16)
    expert_out = lax.psum_scatter(
        jnp.dot(teacher_hidden, outer_weight, preferred_element_type=jnp.float32).astype(
            jnp.bfloat16
        ),
        "dp",
        scatter_dimension=0,
        tiled=True,
    )
    returned = lax.all_to_all(expert_out, "expert", split_axis=0, concat_axis=0, tiled=True)
    picked = jnp.dot(slot_hot, returned, preferred_element_type=jnp.float32).reshape(
        tok_count, 2, tokens.shape[1]
    )
    target = gates[:, 0:1] * picked[:, 0, :] + gates[:, 1:2] * picked[:, 1, :]
    group_tokens = lax.all_gather(tokens, "expert", axis=0, tiled=True)
    preact = jnp.dot(group_tokens, up_proj, preferred_element_type=jnp.float32)
    student_hidden = jax.nn.silu(preact).astype(jnp.bfloat16)
    partial_out = jnp.dot(student_hidden, down_proj, preferred_element_type=jnp.float32)
    student_out = lax.psum_scatter(
        partial_out.astype(jnp.bfloat16), "expert", scatter_dimension=0, tiled=True
    ).astype(jnp.float32)
    scale = 1.0 / jnp.sqrt(jnp.float32(tok_count * n_expert * n_data))
    out_grad = (valid[:, None].astype(jnp.float32) * (student_out - target) * scale).astype(
        jnp.bfloat16
    )
    group_grad = lax.all_gather(out_grad, "expert", axis=0, tiled=True)
    down_term = lax.dot_general(
        student_hidden, group_grad, (((0,), (0,)), ((), ())), preferred_element_type=jnp.float32
    )
    back_hidden = lax.dot_general(
        group_grad, down_proj, (((1,), (1,)), ((), ())), preferred_element_type=jnp.float32
    )
    hidden_grad = (back_hidden * silu_grad(preact)).astype(jnp.bfloat16)
    up_term = lax.dot_general(
        group_tokens, hidden_grad, (((0,), (0,)), ((), ())), preferred_element_type=jnp.float32
    )
    grad_up, grad_down = (
        lax.psum_scatter(
            up_term.astype(jnp.bfloat16), "dp", scatter_dimension=0, tiled=True
        ).astype(jnp.float32),
        lax.psum_scatter(
            down_term.astype(jnp.bfloat16), "dp", scatter_dimension=1, tiled=True
        ).astype(jnp.float32),
    )
    return (grad_up, grad_down)


def solution(mesh):
    return jax.shard_map(
        per_device,
        mesh=mesh,
        in_specs=(
            P(("dp", "expert"), None),
            P(("dp", "expert"), None),
            P(("dp", "expert"), None),
            P(("dp", "expert")),
            P("expert", None, "dp"),
            P("expert", "dp", None),
            P(None, "expert"),
            P("expert", None),
        ),
        out_specs=(P("dp", "expert"), P("expert", "dp")),
        check_vma=False,
    )
```

profile of v0, /device:TPU:1, one launch (start us, length us, event | category | flops | bytes accessed | tf_op | source)
XLA Modules:
  0.0 636.7 jit_solution(16356800401374354791)
XLA Ops:
  8.0 0.0 all-gather.6.cloned.1.call-start
  8.1 0.8 copy.38
  8.9 0.1 eq.51
  9.0 0.1 fusion.19
  9.1 0.1 reduce_window_sum.11
  9.2 0.2 select_reduce_fusion
  9.4 0.1 reduce_sum.12
  9.5 0.1 copy.39
  9.6 0.7 multiply_add_fusion
  10.2 0.1 fusion.23
  10.3 1.2 convolution_convert_fusion.3
  11.6 0.2 reshape.62
  11.8 1.1 copy.40
  12.9 39.0 %all-gather.6.cloned.1.call-done = bf16[8,32,4,2048]{3,1,2,0:T(8,128)(2,1)} async-done(((bf16[1,32,4,2048]{3,1,2,0:T(8,128)(2,1)}), bf16[8,32,4,2048]{3,1,2,0:T(8,128)(2,1)}) %all-gather.6.cloned.1.call-update) | async-done | bytes 4194320 | tf_op jit(solution)/shard_map/all_gather | solution.py:32
  51.9 7.4 %copy.41 = bf16[8,32,4,2048]{3,2,0,1:T(4,128)(2,1)} copy(bf16[8,32,4,2048]{3,1,2,0:T(8,128)(2,1)} %all-gather.6.cloned.1.call-done) | data formatting | bytes 8388608 | tf_op jit(solution)/shard_map/all_gather | solution.py:32
  59.3 9.7 %all-to-all-start = ((bf16[8,32,4,2048]{3,2,0,1:T(4,128)(2,1)}), bf16[8,32,4,2048]{3,2,0,1:T(4,128)(2,1)}, u32[]{:S(2)}, u32[]{:S(2)}) async-start(bf16[8,32,4,2048]{3,2,0,1:T(4,128)(2,1)} %copy.41), calls=%async_computation.1 | async-start | bytes 8388608 | tf_op jit(solution)/shard_map/all_to_all | solution.py:35
  69.0 0.0 all-gather.4.cloned.1.call-start
  69.0 0.5 all-gather.4.cloned.1.call-update
  69.6 0.2 reduce-scatter.7.cloned.1.call-start
  69.8 108.8 %all-to-all-done = bf16[8,32,4,2048]{3,2,0,1:T(4,128)(2,1)} async-done(((bf16[8,32,4,2048]{3,2,0,1:T(4,128)(2,1)}), bf16[8,32,4,2048]{3,2,0,1:T(4,128)(2,1)}, u32[]{:S(2)}, u32[]{:S(2)}) %all-to-all-start) | async-done | bytes 4194336 | tf_op jit(solution)/shard_map/all_to_all | solution.py:35
  178.6 7.1 %copy.42 = bf16[8,32,4,2048]{3,2,1,0:T(4,128)(2,1)} copy(bf16[8,32,4,2048]{3,2,0,1:T(4,128)(2,1)} %all-to-all-done) | data formatting | bytes 8388608 | tf_op jit(solution)/shard_map/all_to_all | solution.py:35
  185.6 6.9 %reshape.63 = bf16[1024,2048]{1,0:T(8,128)(2,1)} reshape(bf16[8,32,4,2048]{3,2,1,0:T(4,128)(2,1)} %copy.42) | data formatting | bytes 8388608 | tf_op jit(solution)/shard_map/reshape | solution.py:36
  192.6 8.1 %maximum_convert_fusion = bf16[1024,1024]{1,0:T(8,128)(2,1)S(1)} fusion(bf16[1024,2048]{1,0:T(8,128)(2,1)} %reshape.63, bf16[1,2048,1024]{2,1,0:T(8,128)(2,1)} %param.12), kind=kOutput, calls=%fused_computation.4 | convolution fusion | flops 4297064448 | bytes 10485760 | tf_op jit(solution)/shard_map/dot_general | solution.py:40
  200.7 6.1 fusion.4
  206.8 0.0 reduce-scatter.5.cloned.1.call-start
  206.9 0.0 all-gather.4.cloned.1.call-done
  206.9 1.1 copy-done.3
  208.0 3.4 fusion.29
  211.5 3.3 convolution_convert_fusion
  214.8 29.4 %reduce-scatter.7.cloned.1.call-done = bf16[128,2048]{1,0:T(8,128)(2,1)} async-done(((bf16[1024,2048]{1,0:T(8,128)(2,1)}), bf16[128,2048]{1,0:T(8,128)(2,1)}) %reduce-scatter.7.cloned.1.call-update) | async-done | bytes 524304 | tf_op jit(solution)/shard_map/reduce_scatter | solution.py:42
  244.1 2.1 all_to_all.16
  246.2 9.5 %all-to-all-start.1 = ((bf16[32,4,2048]{2,1,0:T(4,128)(2,1)}), bf16[32,4,2048]{2,1,0:T(4,128)(2,1)S(1)}, u32[]{:S(2)}, u32[]{:S(2)}) async-start(bf16[32,4,2048]{2,1,0:T(4,128)(2,1)} %all_to_all.16), calls=%async_computation.3 | async-start | bytes 1048576 | tf_op jit(solution)/shard_map/all_to_all | solution.py:50
  255.7 0.0 all-gather.8.cloned.1.call-start
  255.7 12.6 %all-to-all-done.1 = bf16[32,4,2048]{2,1,0:T(4,128)(2,1)S(1)} async-done(((bf16[32,4,2048]{2,1,0:T(4,128)(2,1)}), bf16[32,4,2048]{2,1,0:T(4,128)(2,1)S(1)}, u32[]{:S(2)}, u32[]{:S(2)}) %all-to-all-start.1) | async-done | bytes 524320 | tf_op jit(solution)/shard_map/all_to_all | solution.py:50
  268.4 0.1 reshape.64
  268.5 0.3 fusion.21
  268.8 197.9 %reduce-scatter.5.cloned.1.call-done = bf16[32,2048]{1,0:T(8,128)(2,1)} async-done(((bf16[1024,2048]{1,0:T(8,128)(2,1)}), bf16[32,2048]{1,0:T(8,128)(2,1)}) %reduce-scatter.5.cloned.1.call-update) | async-done | bytes 131088 | tf_op jit(solution)/shard_map/reduce_scatter | solution.py:59
  466.7 1.7 fusion.17
  468.4 0.0 all-gather.8.cloned.1.call-update
  468.4 0.3 reduce-scatter.9.cloned.1.call-start
  468.7 81.8 %all-gather.8.cloned.1.call-done = bf16[1024,2048]{1,0:T(8,128)(2,1)} async-done(((bf16[32,2048]{1,0:T(8,128)(2,1)}), bf16[1024,2048]{1,0:T(8,128)(2,1)}) %all-gather.8.cloned.1.call-update) | async-done | bytes 4194320 | tf_op jit(solution)/shard_map/all_gather | solution.py:66
  550.5 9.0 %fusion.7 = bf16[2048,256]{0,1:T(8,128)(2,1)} fusion(bf16[1024,2048]{1,0:T(8,128)(2,1)} %all-gather.4.cloned.1.call-done, bf16[1024,2048]{1,0:T(8,128)(2,1)} %all-gather.8.cloned.1.call-done, bf16[256,2048]{1,0:T(8,128)(2,1)S(1)} %copy-done, f32[1024,256]{1,0:T(8,128)S(1)} %fusion.29), kind=kOutput, calls=%fused_computation.9 | convolution fusion | flops 2150367232 | bytes 11534336 | tf_op jit(solution)/shard_map/dot_general | solution.py:74
  559.5 0.0 reduce-scatter.11.cloned.1.call-start
  559.6 4.5 convolution_convert_fusion.1
  564.1 28.0 %reduce-scatter.9.cloned.1.call-done = bf16[256,256]{0,1:T(8,128)(2,1)} async-done(((bf16[2048,256]{0,1:T(8,128)(2,1)}), bf16[256,256]{0,1:T(8,128)(2,1)}) %reduce-scatter.9.cloned.1.call-update) | async-done | bytes 131088 | tf_op jit(solution)/shard_map/reduce_scatter | solution.py:78
  592.1 1.7 copy.43
  593.8 34.1 %reduce-scatter.11.cloned.1.call-done = bf16[256,256]{1,0:T(8,128)(2,1)} async-done(((bf16[256,2048]{1,0:T(8,128)(2,1)}), bf16[256,256]{1,0:T(8,128)(2,1)}) %reduce-scatter.11.cloned.1.call-update) | async-done | bytes 131088 | tf_op jit(solution)/shard_map/reduce_scatter | solution.py:81
  627.9 1.6 convert_element_type.65
  (16 shorter events, 0.1 us)
Async XLA Ops:
  8.0 203.5 %copy-start = (bf16[256,2048]{1,0:T(8,128)(2,1)S(1)}, bf16[256,2048]{1,0:T(8,128)(2,1)}, u32[]{:S(2)}) copy-start(bf16[256,2048]{1,0:T(8,128)(2,1)} %param.15) | copy-start | bytes 3145732
  8.0 43.9 %all-gather.6.cloned.1.call-start = ((), (), s32[]{:S(2)}) async-start(), calls=%async_computation.8 | async-start | bytes 4718592 | tf_op jit(solution)/shard_map/all_gather | solution.py:32
  59.3 119.3 %all-to-all-start = ((bf16[8,32,4,2048]{3,2,0,1:T(4,128)(2,1)}), bf16[8,32,4,2048]{3,2,0,1:T(4,128)(2,1)}, u32[]{:S(2)}, u32[]{:S(2)}) async-start(bf16[8,32,4,2048]{3,2,0,1:T(4,128)(2,1)} %copy.41), calls=%async_computation.1 | async-start | bytes 8388608 | tf_op jit(solution)/shard_map/all_to_all | solution.py:35
  69.0 137.9 %all-gather.4.cloned.1.call-start = ((), (), s32[]{:S(2)}) async-start(), calls=%async_computation.6 | async-start | bytes 4325376 | tf_op jit(solution)/shard_map/all_gather | solution.py:55
  69.6 174.6 %reduce-scatter.7.cloned.1.call-start = ((), (), s32[]{:S(2)}) async-start(), calls=%async_computation.9 | async-start | bytes 4718592 | tf_op jit(solution)/shard_map/reduce_scatter | solution.py:42
  192.6 8.1 %copy-start.2 = (bf16[1,1024,2048]{2,1,0:T(8,128)(2,1)S(1)}, bf16[1,1024,2048]{2,1,0:T(8,128)(2,1)}, u32[]{:S(2)}) copy-start(bf16[1,1024,2048]{2,1,0:T(8,128)(2,1)} %param.13) | copy-start | bytes 12582916
  206.8 1.2 copy-start.3
  206.8 259.9 %reduce-scatter.5.cloned.1.call-start = ((), (), s32[]{:S(2)}) async-start(), calls=%async_computation.7 | async-start | bytes 4325376 | tf_op jit(solution)/shard_map/reduce_scatter | solution.py:59
  214.7 41.0 %copy-start.4 = (s32[32]{0:T(128)S(1)}, s32[32]{0:T(128)}, u32[]{:S(2)}) copy-start(s32[32]{0:T(128)} %param.11) | copy-start | bytes 388
  214.7 41.0 %copy-start.1 = (f32[32,2]{0,1:T(2,128)S(1)}, f32[32,2]{0,1:T(2,128)}, u32[]{:S(2)}) copy-start(f32[32,2]{0,1:T(2,128)} %param.10) | copy-start | bytes 772
  246.2 22.2 %all-to-all-start.1 = ((bf16[32,4,2048]{2,1,0:T(4,128)(2,1)}), bf16[32,4,2048]{2,1,0:T(4,128)(2,1)S(1)}, u32[]{:S(2)}, u32[]{:S(2)}) async-start(bf16[32,4,2048]{2,1,0:T(4,128)(2,1)} %all_to_all.16), calls=%async_computation.3 | async-start | bytes 1048576 | tf_op jit(solution)/shard_map/all_to_all | solution.py:50
  255.7 294.8 %all-gather.8.cloned.1.call-start = ((), (), s32[]{:S(2)}) async-start(), calls=%async_computation.10 | async-start | bytes 4325376 | tf_op jit(solution)/shard_map/all_gather | solution.py:66
  468.4 123.7 %reduce-scatter.9.cloned.1.call-start = ((), (), s32[]{:S(2)}) async-start(), calls=%async_computation.11 | async-start | bytes 1179648 | tf_op jit(solution)/shard_map/reduce_scatter | solution.py:78
  559.5 68.4 %reduce-scatter.11.cloned.1.call-start = ((), (), s32[]{:S(2)}) async-start(), calls=%async_computation.12 | async-start | bytes 1179648 | tf_op jit(solution)/shard_map/reduce_scatter | solution.py:81
Sparse Core Ops, SparseCore 0:
  13.0 38.8 all-gather.5
  206.9 37.1 reduce-scatter.6
  248.0 218.6 reduce-scatter.4
  559.7 32.4 reduce-scatter.8
  594.7 33.2 reduce-scatter.10
Sparse Core Ops, SparseCore 1:
  72.0 116.3 all-gather.3
  468.5 81.9 all-gather.7
where the time goes:
time: 639 us; the launch traced here: 637 us
  waiting for transfers between devices  532 us (83%)
  matrix products  35.9 us (6%)
  local copies, waits for them, and re-layouts  28.9 us (5%)
  starting transfers between devices  19.9 us (3%)
  between operations  15.4 us (2%)
    reduce_scatter x1, waiting for transfers between devices, per_device(): lax.psum_scatter(partial_out.astype(jnp.bfloat16), 'expert', scatter_dime...  198 us
    all_to_all x1, waiting for transfers between devices, per_device(): lax.all_to_all(stacked, 'expert', split_axis=1, concat_axis=2, tiled=True)  109 us
    all_gather x1, waiting for transfers between devices, per_device(): group_grad = lax.all_gather(out_grad, 'expert', axis=0, tiled=True)  81.8 us
    all_gather x1, waiting for transfers between devices, per_device(): lax.all_gather(outgoing.reshape(1, n_expert, capacity, tokens.shape[1]),...  39 us
    reduce_scatter x1, waiting for transfers between devices, per_device(): lax.psum_scatter(down_term.astype(jnp.bfloat16), 'dp', scatter_dimension=...  34.1 us
    reduce_scatter x1, waiting for transfers between devices, per_device(): lax.psum_scatter(jnp.dot(teacher_hidden, outer_weight, preferred_element_...  29.4 us
    reduce_scatter x1, waiting for transfers between devices, per_device(): lax.psum_scatter(up_term.astype(jnp.bfloat16), 'dp', scatter_dimension=0,...  28 us
  transfers between devices with their start and end apart: 9, of which 8 were waited for; matrix products, arithmetic and copies ran while one was open for 7% of the time, Pallas kernels for 0%

commit v1 on v0

--- a/solution.py
+++ b/solution.py
@@ -16,10 +16,9 @@
     capacity = 4 * tok_count // n_expert
     slot_width = n_expert * capacity
     flat_ids = expert_ids.reshape(-1)
-    expert_hot = (flat_ids[:, None] == jnp.arange(n_expert, dtype=jnp.int32)[None, :]).astype(
-        jnp.int32
-    )
-    ranks = jnp.sum((jnp.cumsum(expert_hot, axis=0) - 1) * expert_hot, axis=1)
+    order = jnp.arange(flat_ids.shape[0], dtype=jnp.int32)
+    earlier = (flat_ids[:, None] == flat_ids[None, :]) & (order[None, :] < order[:, None])
+    ranks = jnp.sum(earlier.astype(jnp.int32), axis=1)
     slots = flat_ids * capacity + ranks
     slot_hot = (slots[:, None] == jnp.arange(slot_width, dtype=jnp.int32)[None, :]).astype(
         jnp.bfloat16

time: 639 us -> 639 us (level)
  no operation moved by 1% of the time
where the time goes in v1:
time: 639 us; the launch traced here: 637 us
  waiting for transfers between devices  532 us (83%)
  matrix products  35.9 us (6%)
  local copies, waits for them, and re-layouts  28.9 us (5%)
  starting transfers between devices  20 us (3%)
  between operations  15.4 us (2%)
    reduce_scatter x1, waiting for transfers between devices, per_device(): lax.psum_scatter(partial_out.astype(jnp.bfloat16), 'expert', scatter_dime...  198 us
    all_to_all x1, waiting for transfers between devices, per_device(): lax.all_to_all(stacked, 'expert', split_axis=1, concat_axis=2, tiled=True)  109 us
    all_gather x1, waiting for transfers between devices, per_device(): group_grad = lax.all_gather(out_grad, 'expert', axis=0, tiled=True)  81.8 us
    all_gather x1, waiting for transfers between devices, per_device(): lax.all_gather(outgoing.reshape(1, n_expert, capacity, tokens.shape[1]),...  39 us
    reduce_scatter x1, waiting for transfers between devices, per_device(): lax.psum_scatter(down_term.astype(jnp.bfloat16), 'dp', scatter_dimension=...  34.1 us
    reduce_scatter x1, waiting for transfers between devices, per_device(): lax.psum_scatter(jnp.dot(teacher_hidden, outer_weight, preferred_element_...  29.3 us
    reduce_scatter x1, waiting for transfers between devices, per_device(): lax.psum_scatter(up_term.astype(jnp.bfloat16), 'dp', scatter_dimension=0,...  28 us
  transfers between devices with their start and end apart: 9, of which 8 were waited for; matrix products, arithmetic and copies ran while one was open for 7% of the time, Pallas kernels for 0%

profile of v1, /device:TPU:1, one launch (start us, length us, event | category | flops | bytes accessed | tf_op | source)
XLA Modules:
  0.0 636.6 jit_solution(13259199977845364074)
XLA Ops:
  8.0 0.0 all-gather.6.cloned.1.call-start
  8.1 0.8 copy.47
  8.9 0.1 eq.51
  9.0 0.2 convert_reduce_fusion
  9.2 0.1 reduce_sum.12
  9.3 0.1 copy.48
  9.4 0.7 multiply_add_fusion
  10.1 0.1 fusion.23
  10.1 1.2 convolution_convert_fusion.3
  11.4 0.2 reshape.63
  11.6 1.1 copy.49
  12.7 39.0 %all-gather.6.cloned.1.call-done = bf16[8,32,4,2048]{3,1,2,0:T(8,128)(2,1)} async-done(((bf16[1,32,4,2048]{3,1,2,0:T(8,128)(2,1)}), bf16[8,32,4,2048]{3,1,2,0:T(8,128)(2,1)}) %all-gather.6.cloned.1.call-update) | async-done | bytes 4194320 | tf_op jit(solution)/shard_map/all_gather | solution.py:31
  51.7 7.4 %copy.50 = bf16[8,32,4,2048]{3,2,0,1:T(4,128)(2,1)} copy(bf16[8,32,4,2048]{3,1,2,0:T(8,128)(2,1)} %all-gather.6.cloned.1.call-done) | data formatting | bytes 8388608 | tf_op jit(solution)/shard_map/all_gather | solution.py:31
  59.1 9.7 %all-to-all-start = ((bf16[8,32,4,2048]{3,2,0,1:T(4,128)(2,1)}), bf16[8,32,4,2048]{3,2,0,1:T(4,128)(2,1)}, u32[]{:S(2)}, u32[]{:S(2)}) async-start(bf16[8,32,4,2048]{3,2,0,1:T(4,128)(2,1)} %copy.50), calls=%async_computation.1 | async-start | bytes 8388608 | tf_op jit(solution)/shard_map/all_to_all | solution.py:34
  68.8 0.0 all-gather.4.cloned.1.call-start
  68.9 0.5 all-gather.4.cloned.1.call-update
  69.4 0.2 reduce-scatter.7.cloned.1.call-start
  69.6 108.8 %all-to-all-done = bf16[8,32,4,2048]{3,2,0,1:T(4,128)(2,1)} async-done(((bf16[8,32,4,2048]{3,2,0,1:T(4,128)(2,1)}), bf16[8,32,4,2048]{3,2,0,1:T(4,128)(2,1)}, u32[]{:S(2)}, u32[]{:S(2)}) %all-to-all-start) | async-done | bytes 4194336 | tf_op jit(solution)/shard_map/all_to_all | solution.py:34
  178.4 7.1 %copy.51 = bf16[8,32,4,2048]{3,2,1,0:T(4,128)(2,1)} copy(bf16[8,32,4,2048]{3,2,0,1:T(4,128)(2,1)} %all-to-all-done) | data formatting | bytes 8388608 | tf_op jit(solution)/shard_map/all_to_all | solution.py:34
  185.5 7.0 %reshape.64 = bf16[1024,2048]{1,0:T(8,128)(2,1)} reshape(bf16[8,32,4,2048]{3,2,1,0:T(4,128)(2,1)} %copy.51) | data formatting | bytes 8388608 | tf_op jit(solution)/shard_map/reshape | solution.py:35
  192.4 8.1 %maximum_convert_fusion = bf16[1024,1024]{1,0:T(8,128)(2,1)S(1)} fusion(bf16[1024,2048]{1,0:T(8,128)(2,1)} %reshape.64, bf16[1,2048,1024]{2,1,0:T(8,128)(2,1)} %param.12), kind=kOutput, calls=%fused_computation.4 | convolution fusion | flops 4297064448 | bytes 10485760 | tf_op jit(solution)/shard_map/dot_general | solution.py:39
  200.5 6.1 fusion.4
  206.6 0.0 reduce-scatter.7.cloned.1.call-update
  206.7 0.0 reduce-scatter.5.cloned.1.call-start
  206.7 0.0 all-gather.4.cloned.1.call-done
  206.8 1.1 copy-done.3
  207.9 3.4 fusion.29
  211.3 3.3 convolution_convert_fusion
  214.6 0.0 reduce-scatter.5.cloned.1.call-update
  214.6 29.3 %reduce-scatter.7.cloned.1.call-done = bf16[128,2048]{1,0:T(8,128)(2,1)} async-done(((bf16[1024,2048]{1,0:T(8,128)(2,1)}), bf16[128,2048]{1,0:T(8,128)(2,1)}) %reduce-scatter.7.cloned.1.call-update) | async-done | bytes 524304 | tf_op jit(solution)/shard_map/reduce_scatter | solution.py:41
  243.9 2.1 all_to_all.16
  246.0 9.7 %all-to-all-start.1 = ((bf16[32,4,2048]{2,1,0:T(4,128)(2,1)}), bf16[32,4,2048]{2,1,0:T(4,128)(2,1)S(1)}, u32[]{:S(2)}, u32[]{:S(2)}) async-start(bf16[32,4,2048]{2,1,0:T(4,128)(2,1)} %all_to_all.16), calls=%async_computation.3 | async-start | bytes 1048576 | tf_op jit(solution)/shard_map/all_to_all | solution.py:49
  255.6 0.0 all-gather.8.cloned.1.call-start
  255.7 12.6 %all-to-all-done.1 = bf16[32,4,2048]{2,1,0:T(4,128)(2,1)S(1)} async-done(((bf16[32,4,2048]{2,1,0:T(4,128)(2,1)}), bf16[32,4,2048]{2,1,0:T(4,128)(2,1)S(1)}, u32[]{:S(2)}, u32[]{:S(2)}) %all-to-all-start.1) | async-done | bytes 524320 | tf_op jit(solution)/shard_map/all_to_all | solution.py:49
  268.4 0.1 reshape.65
  268.5 0.3 fusion.21
  268.8 197.8 %reduce-scatter.5.cloned.1.call-done = bf16[32,2048]{1,0:T(8,128)(2,1)} async-done(((bf16[1024,2048]{1,0:T(8,128)(2,1)}), bf16[32,2048]{1,0:T(8,128)(2,1)}) %reduce-scatter.5.cloned.1.call-update) | async-done | bytes 131088 | tf_op jit(solution)/shard_map/reduce_scatter | solution.py:58
  466.6 1.7 fusion.17
  468.3 0.0 all-gather.8.cloned.1.call-update
  468.3 0.3 reduce-scatter.9.cloned.1.call-start
  468.6 81.8 %all-gather.8.cloned.1.call-done = bf16[1024,2048]{1,0:T(8,128)(2,1)} async-done(((bf16[32,2048]{1,0:T(8,128)(2,1)}), bf16[1024,2048]{1,0:T(8,128)(2,1)}) %all-gather.8.cloned.1.call-update) | async-done | bytes 4194320 | tf_op jit(solution)/shard_map/all_gather | solution.py:65
  550.4 9.0 %fusion.7 = bf16[2048,256]{0,1:T(8,128)(2,1)} fusion(bf16[1024,2048]{1,0:T(8,128)(2,1)} %all-gather.4.cloned.1.call-done, bf16[1024,2048]{1,0:T(8,128)(2,1)} %all-gather.8.cloned.1.call-done, bf16[256,2048]{1,0:T(8,128)(2,1)S(1)} %copy-done, f32[1024,256]{1,0:T(8,128)S(1)} %fusion.29), kind=kOutput, calls=%fused_computation.9 | convolution fusion | flops 2150367232 | bytes 11534336 | tf_op jit(solution)/shard_map/dot_general | solution.py:73
  559.4 0.0 reduce-scatter.11.cloned.1.call-start
  559.5 4.5 convolution_convert_fusion.1
  564.0 28.0 %reduce-scatter.9.cloned.1.call-done = bf16[256,256]{0,1:T(8,128)(2,1)} async-done(((bf16[2048,256]{0,1:T(8,128)(2,1)}), bf16[256,256]{0,1:T(8,128)(2,1)}) %reduce-scatter.9.cloned.1.call-update) | async-done | bytes 131088 | tf_op jit(solution)/shard_map/reduce_scatter | solution.py:77
  592.0 1.7 copy.52
  593.7 34.1 %reduce-scatter.11.cloned.1.call-done = bf16[256,256]{1,0:T(8,128)(2,1)} async-done(((bf16[256,2048]{1,0:T(8,128)(2,1)}), bf16[256,256]{1,0:T(8,128)(2,1)}) %reduce-scatter.11.cloned.1.call-update) | async-done | bytes 131088 | tf_op jit(solution)/shard_map/reduce_scatter | solution.py:80
  627.8 1.6 convert_element_type.65
  (14 shorter events, 0.1 us)
Async XLA Ops:
  8.0 203.3 %copy-start = (bf16[256,2048]{1,0:T(8,128)(2,1)S(1)}, bf16[256,2048]{1,0:T(8,128)(2,1)}, u32[]{:S(2)}) copy-start(bf16[256,2048]{1,0:T(8,128)(2,1)} %param.15) | copy-start | bytes 3145732
  8.0 43.7 %all-gather.6.cloned.1.call-start = ((), (), s32[]{:S(2)}) async-start(), calls=%async_computation.8 | async-start | bytes 4718592 | tf_op jit(solution)/shard_map/all_gather | solution.py:31
  59.1 119.3 %all-to-all-start = ((bf16[8,32,4,2048]{3,2,0,1:T(4,128)(2,1)}), bf16[8,32,4,2048]{3,2,0,1:T(4,128)(2,1)}, u32[]{:S(2)}, u32[]{:S(2)}) async-start(bf16[8,32,4,2048]{3,2,0,1:T(4,128)(2,1)} %copy.50), calls=%async_computation.1 | async-start | bytes 8388608 | tf_op jit(solution)/shard_map/all_to_all | solution.py:34
  68.8 137.9 %all-gather.4.cloned.1.call-start = ((), (), s32[]{:S(2)}) async-start(), calls=%async_computation.6 | async-start | bytes 4325376 | tf_op jit(solution)/shard_map/all_gather | solution.py:54
  69.4 174.5 %reduce-scatter.7.cloned.1.call-start = ((), (), s32[]{:S(2)}) async-start(), calls=%async_computation.9 | async-start | bytes 4718592 | tf_op jit(solution)/shard_map/reduce_scatter | solution.py:41
  192.4 8.1 %copy-start.2 = (bf16[1,1024,2048]{2,1,0:T(8,128)(2,1)S(1)}, bf16[1,1024,2048]{2,1,0:T(8,128)(2,1)}, u32[]{:S(2)}) copy-start(bf16[1,1024,2048]{2,1,0:T(8,128)(2,1)} %param.13) | copy-start | bytes 12582916
  206.6 1.2 copy-start.3
  206.7 259.9 %reduce-scatter.5.cloned.1.call-start = ((), (), s32[]{:S(2)}) async-start(), calls=%async_computation.7 | async-start | bytes 4325376 | tf_op jit(solution)/shard_map/reduce_scatter | solution.py:58
  214.6 41.1 %copy-start.4 = (s32[32]{0:T(128)S(1)}, s32[32]{0:T(128)}, u32[]{:S(2)}) copy-start(s32[32]{0:T(128)} %param.11) | copy-start | bytes 388
  214.6 41.1 %copy-start.1 = (f32[32,2]{0,1:T(2,128)S(1)}, f32[32,2]{0,1:T(2,128)}, u32[]{:S(2)}) copy-start(f32[32,2]{0,1:T(2,128)} %param.10) | copy-start | bytes 772
  246.0 22.4 %all-to-all-start.1 = ((bf16[32,4,2048]{2,1,0:T(4,128)(2,1)}), bf16[32,4,2048]{2,1,0:T(4,128)(2,1)S(1)}, u32[]{:S(2)}, u32[]{:S(2)}) async-start(bf16[32,4,2048]{2,1,0:T(4,128)(2,1)} %all_to_all.16), calls=%async_computation.3 | async-start | bytes 1048576 | tf_op jit(solution)/shard_map/all_to_all | solution.py:49
  255.6 294.7 %all-gather.8.cloned.1.call-start = ((), (), s32[]{:S(2)}) async-start(), calls=%async_computation.10 | async-start | bytes 4325376 | tf_op jit(solution)/shard_map/all_gather | solution.py:65
  468.3 123.7 %reduce-scatter.9.cloned.1.call-start = ((), (), s32[]{:S(2)}) async-start(), calls=%async_computation.11 | async-start | bytes 1179648 | tf_op jit(solution)/shard_map/reduce_scatter | solution.py:77
  559.4 68.4 %reduce-scatter.11.cloned.1.call-start = ((), (), s32[]{:S(2)}) async-start(), calls=%async_computation.12 | async-start | bytes 1179648 | tf_op jit(solution)/shard_map/reduce_scatter | solution.py:80
Sparse Core Ops, SparseCore 0:
  12.8 38.8 all-gather.5
  206.8 37.0 reduce-scatter.6
  247.8 218.7 reduce-scatter.4
  559.5 32.4 reduce-scatter.8
  594.5 33.2 reduce-scatter.10
Sparse Core Ops, SparseCore 1:
  71.9 116.3 all-gather.3
  468.4 81.9 all-gather.7

commit v2 on v1

v2 whole, which is shorter than its diff:
```python
import functools

import jax
import jax.numpy as jnp
from jax import lax
from jax.experimental import pallas as pl
from jax.experimental.pallas import tpu as pltpu
from jax.sharding import PartitionSpec as P

MESH = pl.DeviceIdType.MESH
CORES = 2
CAP = 4
LANES = 128
F32, BF16 = jnp.float32, jnp.bfloat16


def dot(a, b):
    return jnp.dot(a, b, preferred_element_type=F32)


def dot_nt(a, b):
    return lax.dot_general(a, b, (((1,), (1,)), ((), ())), preferred_element_type=F32)


def run_all(walks):
    walks = list(walks)
    while walks:
        for walk in list(walks):
            try:
                next(walk)
            except StopIteration:
                walks.remove(walk)


def kernel(
    nz, ny, nx, scale,
    tok_ref, ids_ref, gate_ref, valid_ref, win_hbm, wout_hbm, up_hbm, down_hbm,
    gup_ref, gdown_ref,
    win, wout, up, down, grp, rows, hid, part, part_in, xr, eout,
    hstu, hT, sgT, hgT, mix, zr, yr, zs, ys, og, gt, gt_in, gr,
    send_sem, recv_sem, load_sem,
):
    e, g = lax.axis_index("expert"), lax.axis_index("dp")
    z, y = e // ny, lax.rem(e, ny)
    x, c = g // CORES, lax.rem(g, CORES)
    tok, width = tok_ref.shape
    half = tok // 2
    group = nz * ny * tok
    slots = nz * ny * CAP
    hidden = hstu.shape[1]
    ffw = hid.shape[1]

    def at_z(k):
        return (lax.rem(z + k, nz) * ny + y, g)

    def at_y(k):
        return (z * ny + lax.rem(y + k, ny), g)

    def at_x(k):
        return (e, lax.rem(x + k, nx) * CORES + c)

    sibling = (e, x * CORES + 1 - c)

    loads = [
        pltpu.make_async_copy(up_hbm, up, load_sem.at[0]),
        pltpu.make_async_copy(win_hbm.at[0], win, load_sem.at[1]),
        pltpu.make_async_copy(wout_hbm.at[0], wout, load_sem.at[2]),
        pltpu.make_async_copy(down_hbm, down, load_sem.at[3]),
    ]
    for load in loads:
        load.start()

    barrier = pltpu.get_barrier_semaphore()
    near = [sibling]
    near += [at_z(k) for k in sorted({1, nz - 1})]
    near += [at_y(k) for k in range(1, ny)]
    near += [at_x(k) for k in sorted({1, nx - 1})]
    for device in near:
        pl.semaphore_signal(barrier, inc=1, device_id=device, device_id_type=MESH)

    lane = lax.broadcasted_iota(jnp.int32, (tok, LANES), 1)
    expert, kind = lane & 31, lane >> 5
    first, second = ids_ref[:, 0:1] == expert, ids_ref[:, 1:2] == expert
    hot = jnp.where(first | second, 1.0, 0.0)
    below = lax.broadcasted_iota(jnp.int32, (tok, tok), 1) < lax.broadcasted_iota(jnp.int32, (tok, tok), 0)
    rank = dot(jnp.where(below, 1.0, 0.0).astype(BF16), hot.astype(BF16))
    gate = jnp.where(first, gate_ref[:, 0:1], 0.0) + jnp.where(second, gate_ref[:, 1:2], 0.0)
    high = gate.astype(BF16).astype(F32)
    table = jnp.where(
        kind == 0, hot * (1.0 + rank), jnp.where(kind == 1, high, jnp.where(kind == 2, gate - high, 0.0))
    )
    grp[z, y, :, 0:width] = tok_ref[...]
    grp[z, y, :, width : width + LANES] = table.astype(BF16)

    pl.semaphore_wait(barrier, len(near))

    sent, count = [], [0]

    def send(src, dst, device):
        k = count[0]
        count[0] += 1
        copy = pltpu.make_async_remote_copy(
            src_ref=src, dst_ref=dst, send_sem=send_sem.at[k], recv_sem=recv_sem.at[k],
            device_id=device, device_id_type=MESH,
        )
        copy.start()
        sent.append(copy)
        return copy

    def ring_gather(n, i, way, at, region, arrived=None):
        last = None
        for s in range(1, n // 2 + 1):
            place = lax.rem(i + n - way * (s - 1), n)
            if last is not None:
                yield
                last.wait_recv()
                if arrived is not None:
                    arrived(place, None)
            cut = None if s < n // 2 else (0 if way == 1 else 1)
            ref = region(place, cut)
            last = send(ref, ref, at(1 if way == 1 else n - 1))
        yield
        last.wait_recv()
        if arrived is not None:
            arrived(lax.rem(i + n // 2, n), 0 if way == 1 else 1)

    def ring_sum(n, i, way, at, own, landing, add):
        last, cut = None, None
        for s in range(1, n // 2 + 1):
            place = lax.rem(i + n + way * (n // 2 - s + 1), n)
            if last is not None:
                yield
                last.wait_recv()
                add(own(place, cut), landing(s - 2, cut))
            cut = None if s > 1 else (0 if way == 1 else 1)
            last = send(own(place, cut), landing(s - 1, cut), at(1 if way == 1 else n - 1))
        yield
        last.wait_recv()
        add(own(i, cut), landing(n // 2 - 1, cut))

    def add_into(a, b):
        a[...] = (a[...].astype(F32) + b[...].astype(F32)).astype(BF16)

    def split(ref, cut, dim):
        if cut is None:
            return ref
        n = ref.shape[dim]
        low = n // 2 // LANES * LANES if dim == len(ref.shape) - 1 else n // 2
        where = pl.ds(0, low) if cut == 0 else pl.ds(low, n - low)
        return ref.at[tuple([slice(None)] * dim + [where])]

    upper, lower = pl.ds(0, half), pl.ds(half, half)

    def gather_plane(buf):
        def upper_first():
            mine = buf.at[z, y, upper, :]
            copies = [send(mine, mine, at_y(k)) for k in range(1, ny)]
            yield
            for copy in copies:
                copy.wait_recv()
            region = lambda p, cut: split(buf.at[p, :, upper, :], cut, 0)
            ways = [ring_gather(nz, z, w, at_z, region) for w in (1, -1)]
            yield from both(ways)

        def lower_first():
            region = lambda p, cut: split(buf.at[p, y, lower, :], cut, 1)
            yield from both([ring_gather(nz, z, w, at_z, region) for w in (1, -1)])
            region = lambda p, cut: split(buf.at[:, p, lower, :], cut, 0)
            yield from both([ring_gather(ny, y, w, at_y, region) for w in (1, -1)])

        run_all([upper_first(), lower_first()])

    def both(walks):
        while walks:
            for walk in list(walks):
                try:
                    next(walk)
                except StopIteration:
                    walks.remove(walk)
            if walks:
                yield

    with jax.named_scope("tokens_gather"):
        gather_plane(grp)

    tab = lambda: grp[:, :, :, width : width + LANES].reshape(group, LANES)
    with jax.named_scope("select"):
        pick = jnp.where(lax.broadcasted_iota(jnp.int32, (16, LANES), 1) == e, 1.0, 0.0).astype(BF16)
        ranks_row = dot_nt(pick, tab())[0:1, :]
        slot = lax.broadcasted_iota(jnp.int32, (slots, group), 0)
        token = lax.broadcasted_iota(jnp.int32, (slots, group), 1)
        wanted = ((slot & (CAP - 1)) + 1).astype(F32)
        chosen = (slot // CAP == token // tok) & (ranks_row == wanted)
        select = jnp.where(chosen, 1.0, 0.0).astype(BF16)
        tile = min(512, width)
        for j in range(width // tile):
            cols = slice(j * tile, (j + 1) * tile)
            rows[x, c, :, cols] = dot(select, grp[:, :, :, cols].reshape(group, tile)).astype(BF16)

    from_sibling = []

    def to_sibling(p, cut):
        ref = split(rows.at[p, c], cut, 0)
        from_sibling.append(send(ref, ref, sibling))

    to_sibling(x, None)
    gathers = [
        ring_gather(nx, x, w, at_x, lambda p, cut: split(rows.at[p, c], cut, 0), to_sibling) for w in (1, -1)
    ]
    for walk in gathers:
        next(walk)

    with jax.named_scope("student_forward"):
        loads[0].wait()
        step = 2 * ny * tok if nz % 2 == 0 else ny * tok

        @pl.loop(0, group // step)
        def _(k):
            block = grp[pl.ds(k * (step // (ny * tok)), step // (ny * tok)), :, :, 0:width].reshape(step, width)
            value = dot(block, up[...])
            place = pl.multiple_of(k * step, step)
            sig = jax.nn.sigmoid(value)
            hstu[pl.ds(place, step), :] = (value * sig).astype(BF16)
            hT[:, pl.ds(place, step)] = (value * sig).T.astype(BF16)
            sgT[:, pl.ds(place, step)] = (sig * (1.0 + value * (1.0 - sig))).T

    loads[1].wait()
    loads[2].wait()

    def teacher(p):
        tile = min(256, ffw)

        @pl.loop(0, ffw // tile)
        def _(j):
            cols = pl.ds(pl.multiple_of(j * tile, tile), tile)
            value = dot(rows[p].reshape(CORES * slots, width), win[:, cols])
            hid[:, cols] = jnp.maximum(value, 0.0).astype(BF16)

        tile2 = min(256, width)

        @pl.loop(0, width // tile2)
        def _(j):
            cols = pl.ds(pl.multiple_of(j * tile2, tile2), tile2)
            value = dot(hid[...], wout[:, cols])
            part[p, :, :, cols] = value.astype(BF16).reshape(CORES, slots, tile2)

    with jax.named_scope("teacher"):
        run_all(gathers)
        for copy in from_sibling:
            copy.wait_recv()
        order = [lax.rem(x + k, nx) for k in ([nx // 2] + [k for k in range(1, nx) if k != nx // 2] + [0])]
        swaps = []
        for p in order:
            teacher(p)
            swaps.append(send(part.at[p, 1 - c], part_in.at[p], sibling))
        for p, swap in zip(order, swaps):
            swap.wait_recv()
            add_into(part.at[p, c], part_in.at[p])
        run_all([
            ring_sum(
                nx, x, w, at_x, lambda p, cut: split(part.at[p, c], cut, 0),
                lambda s, cut, w=w: split(xr.at[(1 - w) // 2, s], cut, 0), add_into,
            )
            for w in (1, -1)
        ])
        eout[...] = part[x, c]

    with jax.named_scope("combine"):
        loads[3].wait()
        blocks = step // (ny * tok)
        tile = min(512, width)
        row = lax.broadcasted_iota(jnp.int32, (LANES, slots), 0)
        pick_rank = jnp.where(row == e, 1.0, 0.0).astype(BF16)
        pick_gate = jnp.where((row == e + 32) | (row == e + 64), 1.0, 0.0).astype(BF16)

        @pl.loop(0, group // step)
        def _(k):
            tab_k = grp[pl.ds(k * blocks, blocks), :, :, width : width + LANES].reshape(step, LANES)
            ranks = dot(tab_k, pick_rank)
            gates = dot(tab_k, pick_gate)
            token = lax.broadcasted_iota(jnp.int32, (step, slots), 0) + k * step
            slot = lax.broadcasted_iota(jnp.int32, (step, slots), 1)
            chosen = (slot // CAP == token // tok) & (ranks == ((slot & (CAP - 1)) + 1).astype(F32))
            back = jnp.where(chosen, 1.0, 0.0).astype(BF16)
            place = pl.multiple_of(k * step, step)
            for j in range(width // tile):
                cols = slice(j * tile, (j + 1) * tile)
                value = dot(hstu[pl.ds(place, step), :], down[:, cols])
                value = value - gates[:, 0:1] * dot(back, eout[:, cols])
                mix[pl.ds(k * blocks, blocks), :, :, cols] = value.astype(BF16).reshape(blocks, ny, tok, tile)

    def sum_upper():
        yield from both([
            ring_sum(
                nz, z, w, at_z, lambda p, cut: split(mix.at[p, :, upper, :], cut, 0),
                lambda s, cut, w=w: split(zr.at[(1 - w) // 2, s], cut, 0), add_into,
            )
            for w in (1, -1)
        ])
        copies = []
        for k in range(1, ny):
            to = lax.rem(y + k, ny)
            copies.append(send(mix.at[z, to, upper, :], ys.at[k - 1], at_y(k)))
        yield
        for copy in copies:
            copy.wait_recv()

    def sum_lower():
        yield from both([
            ring_sum(
                ny, y, w, at_y, lambda p, cut: split(mix.at[:, p, lower, :], cut, 0),
                lambda s, cut, w=w: split(yr.at[(1 - w) // 2, s], cut, 0), add_into,
            )
            for w in (1, -1)
        ])
        yield from both([
            ring_sum(
                nz, z, w, at_z, lambda p, cut: split(mix.at[p, y, lower, :], cut, 1),
                lambda s, cut, w=w: split(zs.at[(1 - w) // 2, s], cut, 1), add_into,
            )
            for w in (1, -1)
        ])

    with jax.named_scope("output_sum"):
        run_all([sum_upper(), sum_lower()])
        weight = valid_ref[...].astype(F32) * scale
        value = mix[z, y, 0:half, :].astype(F32)
        for k in range(ny - 1):
            value = value + ys[k].astype(F32)
        og[z, y, 0:half, :] = (weight[0:half] * value).astype(BF16)
        og[z, y, half:tok, :] = (weight[half:tok] * mix[z, y, half:tok, :].astype(F32)).astype(BF16)

    with jax.named_scope("grad_gather"):
        gather_plane(og)

    with jax.named_scope("backward"):
        share = width // (nx * CORES)

        @pl.loop(0, nx * CORES)
        def _(k):
            cols = pl.ds(pl.multiple_of(k * share, share), share)
            value = dot(hT[...], og[:, :, :, cols].reshape(group, share))
            gt[k // CORES, lax.rem(k, CORES), 1] = value.astype(BF16)

        swap_down = send(gt.at[:, 1 - c, 1], gt_in.at[:, 1], sibling)

        @pl.loop(0, group // step)
        def _(k):
            block = og[pl.ds(k * blocks, blocks)].reshape(step, width)
            place = pl.ds(pl.multiple_of(k * step, step), step)
            hgT[:, place] = (dot_nt(down[...], block) * sgT[:, place]).astype(BF16)

        @pl.loop(0, nx * CORES)
        def _(k):
            cols = pl.ds(pl.multiple_of(k * share, share), share)
            value = dot(hgT[...], grp[:, :, :, cols].reshape(group, share))
            gt[k // CORES, lax.rem(k, CORES), 0] = value.astype(BF16)

        swap_up = send(gt.at[:, 1 - c, 0], gt_in.at[:, 0], sibling)
        swap_down.wait_recv()
        swap_up.wait_recv()
        for p in range(nx):
            add_into(gt.at[p, c], gt_in.at[p])
        run_all([
            ring_sum(
                nx, x, w, at_x, lambda p, cut: split(gt.at[p, c], cut, 0),
                lambda s, cut, w=w: split(gr.at[(1 - w) // 2, s], cut, 0), add_into,
            )
            for w in (1, -1)
        ])
        gup_ref[...] = gt[x, c, 0].astype(F32).T
        gdown_ref[...] = gt[x, c, 1].astype(F32)

    for copy in sent:
        copy.wait_send()


def per_device(nz, ny, nx, tokens, expert_ids, gates, valid, w_in, w_out, up_proj, down_proj):
    tok, width = tokens.shape
    ffw, hidden = w_in.shape[2], up_proj.shape[1]
    group = nz * ny * tok
    slots = nz * ny * CAP
    half = tok // 2
    share = width // (nx * CORES)
    scale = 1.0 / float(group * nx * CORES) ** 0.5
    copies = 160
    vmem = lambda shape, dtype=BF16: pltpu.VMEM(shape, dtype)
    scratch = [
        vmem((width, ffw)), vmem((ffw, width)), vmem((width, hidden)), vmem((hidden, width)),
        vmem((nz, ny, tok, width + LANES)),
        vmem((nx, CORES, slots, width)),
        vmem((CORES * slots, ffw)),
        vmem((nx, CORES, slots, width)),
        vmem((nx, slots, width)),
        vmem((2, nx // 2, slots, width)),
        vmem((slots, width)),
        vmem((group, hidden)),
        vmem((hidden, group)), vmem((hidden, group), F32), vmem((hidden, group)),
        vmem((nz, ny, tok, width)),
        vmem((2, nz // 2, ny, half, width)),
        vmem((2, ny // 2, nz, half, width)),
        vmem((2, nz // 2, half, width)),
        vmem((max(ny - 1, 1), half, width)),
        vmem((nz, ny, tok, width)),
        vmem((nx, CORES, 2, hidden, share)),
        vmem((nx, 2, hidden, share)),
        vmem((2, nx // 2, 2, hidden, share)),
        pltpu.SemaphoreType.DMA((copies,)),
        pltpu.SemaphoreType.DMA((copies,)),
        pltpu.SemaphoreType.DMA((4,)),
    ]
    in_vmem = pl.BlockSpec(memory_space=pltpu.VMEM)
    anywhere = pl.BlockSpec(memory_space=pl.ANY)
    return pl.pallas_call(
        functools.partial(kernel, nz, ny, nx, scale),
        out_shape=(
            jax.ShapeDtypeStruct((share, hidden), F32),
            jax.ShapeDtypeStruct((hidden, share), F32),
        ),
        in_specs=[in_vmem] * 4 + [anywhere] * 4,
        out_specs=(in_vmem, in_vmem),
        scratch_shapes=scratch,
        cost_estimate=pl.CostEstimate(flops=15 * 10**9, bytes_accessed=11 * 10**6, transcendentals=0),
        compiler_params=pltpu.CompilerParams(
            collective_id=0, has_side_effects=True, vmem_limit_bytes=60 * 2**20
        ),
    )(tokens, expert_ids, gates, valid.reshape(tok, 1), w_in, w_out, up_proj, down_proj)


def solution(mesh):
    n_expert, n_dp = mesh.shape["expert"], mesh.shape["dp"]
    ny = 4 if n_expert >= 16 else 2
    nz, nx = n_expert // ny, n_dp // CORES
    return jax.shard_map(
        functools.partial(per_device, nz, ny, nx),
        mesh=mesh,
        in_specs=(
            P(("dp", "expert"), None),
            P(("dp", "expert"), None),
            P(("dp", "expert"), None),
            P(("dp", "expert")),
            P("expert", None, "dp"),
            P("expert", "dp", None),
            P(None, "expert"),
            P("expert", None),
        ),
        out_specs=(P("dp", "expert"), P("expert", "dp")),
        check_vma=False,
    )
```

time: 639 us -> 230 us (0.36)
  waiting for transfers between devices: 532 us -> 0 us
  Pallas kernels: 0 us -> 222 us
  matrix products: 35.9 us -> 0 us
  local copies, waits for them, and re-layouts: 28.9 us -> 7.4 us
  starting transfers between devices: 20 us -> 0 us
  between operations: 15.4 us -> 0.64 us
    reduce_scatter x4 -> x0, waiting for transfers between devices: 289 us -> none  [the longest x1 198 us: per_device(): lax.psum_scatter(partial_out.astype(jnp.bfloat16), 'expert', scatter_dime...]
    pallas_call x0 -> x1, Pallas kernels: none -> 222 us  [per_device(): pl.pallas_call(functools.partial(kernel, nz, ny, nx, scale), out_shape=(j...]
    all_to_all x2 -> x0, waiting for transfers between devices: 121 us -> none  [the longest x1 109 us: per_device(): lax.all_to_all(stacked, 'expert', split_axis=1, concat_axis=2, tiled=True)]
    all_gather x3 -> x0, waiting for transfers between devices: 121 us -> none  [the longest x1 81.8 us: per_device(): group_grad = lax.all_gather(out_grad, 'expert', axis=0, tiled=True)]
    dot_general x8 -> x0, matrix products: 35.9 us -> none  [the longest x1 9.04 us: per_device(): lax.dot_general(group_tokens, hidden_grad, (((0,), (0,)), ((), ())), pref...]
    all_to_all x2 -> x0, starting transfers between devices: 19.4 us -> none  [the longest x1 9.7 us: per_device(): lax.all_to_all(stacked, 'expert', split_axis=1, concat_axis=2, tiled=True)]
    all_to_all x3 -> x0, local copies, waits for them, and re-layouts: 9.26 us -> none  [the longest x1 7.08 us: per_device(): lax.all_to_all(stacked, 'expert', split_axis=1, concat_axis=2, tiled=True)]
    all_gather x1 -> x0, local copies, waits for them, and re-layouts: 7.4 us -> none  [per_device(): lax.all_gather(outgoing.reshape(1, n_expert, capacity, tokens.shape[1]),...]
  transfers between devices with their start and end apart: 9 -> 0, of which waited for: 8 -> 0; matrix products, arithmetic and copies ran while one was open for 7% -> 0% of each run, Pallas kernels for 0% -> 0%
where the time goes in v2:
time: 230 us
  Pallas kernels  222 us (97%)
  local copies, waits for them, and re-layouts  7.4 us (3%)
    pallas_call x1, Pallas kernels, per_device(): pl.pallas_call(functools.partial(kernel, nz, ny, nx, scale), out_shape=(j...  222 us
    unnamed x4, local copies, waits for them, and re-layouts  6.07 us

profile of v2, /device:TPU:1, one launch (start us, length us, event | category | flops | bytes accessed | tf_op | source)
XLA Modules:
  0.0 230.0 jit_solution(12881181615354578608)
XLA Ops:
  0.6 1.4 copy.10.ids_ref
  2.0 1.4 copy.11.gate_ref
  3.4 1.3 copy.12.valid_ref
  4.7 221.9 %shard_map.95 = (f32[256,256]{1,0:T(8,128)}, f32[256,256]{1,0:T(8,128)}) custom-call(bf16[32,2048]{1,0:T(8,128)(2,1)} %tok_ref.1, s32[32,2]{1,0:T(8,128)} %copy.10.ids_ref, f32[32,2]{1,0:T(8,128)} %copy.11.gate_ref, s32[32,1]{1,0:T(8,128)} %copy.12.valid_ref, bf16[1,2048,1024]{2,1,0:T(8,128)(2,1)} %win_hbm.1, bf16[1,1024,2048]{2,1,0:T(8,128)(2,1)} %wout_hbm.1, ...), custom_call_target="tpu_custom_call" | custom-call | flops 15000000512 | bytes 11000000 | tf_op jit(solution)/shard_map/pallas_call | solution.py:414
  226.7 1.7 copy.15
  228.3 1.7 copy.16

commit v3 on v1

v3 whole, which is shorter than its diff:
```python
import functools

import jax
import jax.numpy as jnp
from jax import lax
from jax.experimental import pallas as pl
from jax.experimental.pallas import tpu as pltpu
from jax.sharding import PartitionSpec as P

MESH = pl.DeviceIdType.MESH
CORES = 2
CAP = 4
LANES = 128
Z_FIRST = 0
F32, BF16 = jnp.float32, jnp.bfloat16


def dot(a, b):
    return jnp.dot(a, b, preferred_element_type=F32)


def dot_nt(a, b):
    return lax.dot_general(a, b, (((1,), (1,)), ((), ())), preferred_element_type=F32)


class Event:
    def __init__(self):
        self.done = False


class Work:
    def __init__(self, us, rank=0):
        self.us, self.rank = us, rank


class Plan:
    RATE, INNER, LATENCY = 100e3, 400e3, 2.2

    def __init__(self):
        self.now, self.busy, self.processes = 0.0, {}, []

    def transfer(self, link, nbytes):
        start = max(self.now, self.busy.get(link, 0.0))
        self.busy[link] = start + nbytes / (self.INNER if link == "core" else self.RATE / CORES)
        return self.busy[link] + self.LATENCY

    def spawn(self, process):
        self.processes.append([process, self.now])

    def run(self):
        while self.processes:
            ready, works, later = [], [], []
            for i, (_, want) in enumerate(self.processes):
                if isinstance(want, Event):
                    if want.done:
                        ready.append((self.now, i))
                elif isinstance(want, Work):
                    works.append((want.rank, i))
                elif want <= self.now:
                    ready.append((want, i))
                else:
                    later.append((want, i))
            if ready:
                i = min(ready)[1]
            elif works:
                i = min(works)[1]
                self.now += self.processes[i][1].us
            else:
                self.now, i = min(later)
            process = self.processes[i]
            try:
                process[1] = next(process[0])
            except StopIteration:
                self.processes.remove(process)


def add_into(a, b):
    a[...] = (a[...].astype(F32) + b[...].astype(F32)).astype(BF16)


def kernel(
    nz, ny, nx, scale, n_part,
    tok_ref, ids_ref, gate_ref, valid_ref, win_hbm, wout_hbm, up_hbm, down_hbm,
    gup_ref, gdown_ref,
    win, wout, up, down, grp, rows, acc, hid, part, part_in, xr, eout,
    hstu, hT, sgT, hgT, back, mix, zr, yr, zs, ys, og, gt, gt_in, gr,
    send_sem, recv_sem, load_sem,
):
    e, g = lax.axis_index("expert"), lax.axis_index("dp")
    z, y = e // ny, lax.rem(e, ny)
    x, c = g // CORES, lax.rem(g, CORES)
    tok, width = tok_ref.shape
    group = nz * ny * tok
    slots = nz * ny * CAP
    ffw = win.shape[1]
    wide = width // n_part
    share = width // (nx * CORES)

    def at_z(k):
        return (lax.rem(z + k, nz) * ny + y, g)

    def at_y(k):
        return (z * ny + lax.rem(y + k, ny), g)

    def at_x(k):
        return (e, lax.rem(x + k, nx) * CORES + c)

    sibling = (e, x * CORES + 1 - c)
    ring_z, ring_y, ring_x = (nz, z, at_z, "z"), (ny, y, at_y, "y"), (nx, x, at_x, "x")

    loads = [
        pltpu.make_async_copy(win_hbm.at[0], win, load_sem.at[0]),
        pltpu.make_async_copy(up_hbm, up, load_sem.at[1]),
        pltpu.make_async_copy(wout_hbm.at[0], wout, load_sem.at[2]),
        pltpu.make_async_copy(down_hbm, down, load_sem.at[3]),
    ]

    barrier = pltpu.get_barrier_semaphore()
    near = [sibling]
    near += [at_z(k) for k in sorted({1, nz - 1})]
    near += [at_y(k) for k in range(1, ny)]
    near += [at_x(k) for k in sorted({1, nx - 1})]
    for device in near:
        pl.semaphore_signal(barrier, inc=1, device_id=device, device_id_type=MESH)
    for load in loads:
        load.start()

    row = lax.broadcasted_iota(jnp.int32, (LANES, tok), 0)
    expert, kind = row & 31, row >> 5
    first, second = ids_ref[0:1, :] == expert, ids_ref[1:2, :] == expert
    hot = jnp.where(first | second, 1.0, 0.0)
    before = lax.broadcasted_iota(jnp.int32, (tok, tok), 0) < lax.broadcasted_iota(jnp.int32, (tok, tok), 1)
    rank = dot(hot.astype(BF16), jnp.where(before, 1.0, 0.0).astype(BF16))
    gate = jnp.where(first, gate_ref[0:1, :], 0.0) + jnp.where(second, gate_ref[1:2, :], 0.0)
    high = gate.astype(BF16).astype(F32)
    table = jnp.where(kind == 0, hot * (1.0 + rank), jnp.where(kind == 1, high, gate - high))
    table = jnp.where(kind == 3, valid_ref[...].astype(F32), table)
    grp[z, y, :, 0:LANES] = table.T.astype(BF16)
    grp[z, y, :, LANES : LANES + width] = tok_ref[...]

    pl.semaphore_wait(barrier, len(near))

    plan = Plan()
    sent = []

    def send(src, dst, device, link):
        k = len(sent)
        copy = pltpu.make_async_remote_copy(
            src_ref=src, dst_ref=dst, send_sem=send_sem.at[k], recv_sem=recv_sem.at[k],
            device_id=device, device_id_type=MESH,
        )
        copy.start()
        size = 2
        for n in src.shape:
            size *= n
        sent.append(copy)
        return copy, plan.transfer(link, size)

    def ring_gather(ring, way, region, done, far, arrived=None):
        n, i, at, name = ring
        steps = n // 2 if way == far else n // 2 - 1
        for s in range(1, steps + 1):
            ref = region(lax.rem(i + n - way * (s - 1), n))
            copy, due = send(ref, ref, at(1 if way == 1 else n - 1), name + str(way))
            yield due
            copy.wait_recv()
            if arrived is not None:
                arrived(way * s)
        done.done = True

    def ring_sum(ring, way, own, landing, done, far, us):
        n, i, at, name = ring
        steps = n // 2 if way == far else n // 2 - 1
        for s in range(1, steps + 1):
            place = lax.rem(i + n + way * (steps - s + 1), n)
            copy, due = send(own(place), landing(s - 1), at(1 if way == 1 else n - 1), name + str(way))
            yield due
            copy.wait_recv()
            add_into(own(lax.rem(i + n + way * (steps - s), n)), landing(s - 1))
            plan.now += us
        done.done = True

    def both_ways(start):
        ends = []
        for way in (1, -1):
            ends.append(Event())
            plan.spawn(start(way, ends[-1]))
        return ends

    def all_of(events, done):
        for event in events:
            yield event
        done.done = True

    def y_then_z(buf, cols, done):
        ends = []

        def along_z(k):
            far = 1 if k in (0, 1) else -1
            region = lambda p: buf.at[p, lax.rem(y + ny - k, ny), :, cols]
            ends.extend(both_ways(lambda w, end: ring_gather(ring_z, w, region, end, far)))

        mine = buf.at[z, y, :, cols]
        hops = sorted(range(1, ny), key=lambda k: min(k, ny - k))
        copies = [(k, *send(mine, mine, at_y(k), "y1" if k <= ny // 2 else "y-1")) for k in hops]
        along_z(0)
        for k, copy, due in copies:
            yield due
            copy.wait_recv()
            along_z(k)
        plan.spawn(all_of(ends, done))

    def z_then_y(buf, cols, done):
        ends = []

        def along_y(k):
            far = 1 if len(ends) % 4 == 0 else -1
            region = lambda p: buf.at[lax.rem(z + nz - k, nz), p, :, cols]
            ends.extend(both_ways(lambda w, end: ring_gather(ring_y, w, region, end, far)))

        region = lambda p: buf.at[p, y, :, cols]
        firsts = both_ways(lambda w, end: ring_gather(ring_z, w, region, end, 1, along_y))
        along_y(0)
        for end in firsts:
            yield end
        plan.spawn(all_of(ends, done))

    def columns(q, shift):
        return pl.ds(q * wide + (shift if q else 0), wide + (0 if q else shift))

    def gather_plane(buf, q, shift, done):
        return (z_then_y if q == Z_FIRST else y_then_z)(buf, columns(q, shift), done)

    def sum_z_then_y(q, cols, done):
        from_y = []

        def along_z(k):
            to = lax.rem(y + k, ny)
            own = lambda p: mix.at[p, to, :, cols]
            landing = lambda w: lambda s: zr.at[k, (1 - w) // 2, s]
            far = 1 if k in (0, 1) else -1
            for end in both_ways(lambda w, end: ring_sum(ring_z, w, own, landing(w), end, far, 0.1)):
                yield end
            if k:
                from_y.append(
                    send(mix.at[z, to, :, cols], ys.at[k - 1], at_y(k), "y1" if k <= ny // 2 else "y-1")
                )
            finished[k].done = True

        finished = [Event() for _ in range(ny)]
        for k in sorted(range(ny), key=lambda k: -min(k, ny - k)):
            plan.spawn(along_z(k))
        for event in finished:
            yield event
        for copy, due in from_y:
            yield due
            copy.wait_recv()
        done.done = True

    def sum_y_then_z(q, cols, done):
        finished = [Event() for _ in range(nz)]

        def along_y(k, far):
            to = lax.rem(z + k, nz)
            own = lambda p: mix.at[to, p, :, cols]
            landing = lambda w: lambda s: yr.at[k, (1 - w) // 2, s]
            for end in both_ways(lambda w, end: ring_sum(ring_y, w, own, landing(w), end, far, 0.1)):
                yield end
            finished[k].done = True

        def along_z(way, end):
            n, i, at, name = ring_z
            steps = n // 2 if way == 1 else n // 2 - 1
            for s in range(1, steps + 1):
                k = steps - s + 1
                yield finished[(way * k) % n]
                copy, due = send(
                    mix.at[lax.rem(i + n + way * k, n), y, :, cols], zs.at[(1 - way) // 2, s - 1],
                    at(1 if way == 1 else n - 1), name + str(way),
                )
                yield due
                copy.wait_recv()
                yield finished[(way * (k - 1)) % n]
                add_into(mix.at[lax.rem(i + n + way * (k - 1), n), y, :, cols], zs.at[(1 - way) // 2, s - 1])
                plan.now += 0.1
            end.done = True

        for at, k in enumerate(sorted(range(nz), key=lambda k: -min(k, nz - k))):
            plan.spawn(along_y(k, 1 if at % 2 == 0 else -1))
        for end in both_ways(along_z):
            yield end
        done.done = True

    each = lambda: [Event() for _ in range(n_part)]
    gathered, selected, hidden, summed, mixed, out, grads = each(), each(), each(), each(), each(), each(), each()
    student = Event()
    part_cols = lambda q: pl.ds(q * wide, wide)
    hops = nx // 2
    order = [nx // 2] + [k for k in range(1, nx) if k != nx // 2] + [0]
    whole = [[Event() for _ in range(nx)] for _ in range(n_part)]
    multiplied = [[Event() for _ in range(nx)] for _ in range(n_part)]

    def take_slots(q):
        if q:
            yield selected[q - 1]
        yield gathered[q]
        pick = jnp.where(lax.broadcasted_iota(jnp.int32, (16, LANES), 1) == e, 1.0, 0.0).astype(BF16)
        ranks_row = dot_nt(pick, grp[:, :, :, 0:LANES].reshape(group, LANES))[0:1, :]
        slot = lax.broadcasted_iota(jnp.int32, (slots, group), 0)
        token = lax.broadcasted_iota(jnp.int32, (slots, group), 1)
        chosen = (slot // CAP == token // tok) & (ranks_row == ((slot & (CAP - 1)) + 1).astype(F32))
        select = jnp.where(chosen, 1.0, 0.0).astype(BF16)
        tile = min(512, wide)
        for j in range(wide // tile):
            at = q * wide + j * tile
            block = grp[:, :, :, LANES + at : LANES + at + tile].reshape(group, tile)
            rows[x, c, :, at : at + tile] = dot(select, block).astype(BF16)
        plan.now += 0.6
        selected[q].done = True
        cols = part_cols(q)
        fromsib = {k: [] for k in range(nx)}
        low, high = pl.ds(0, slots // 2), pl.ds(slots // 2, slots // 2)

        def to_sibling(k, p, where):
            ref = rows.at[p, c, where, cols]
            fromsib[k].append(send(ref, ref, sibling, "core"))
            if len(fromsib[k]) == (2 if k else 1):
                plan.spawn(settle(k))

        def settle(k):
            for copy, due in fromsib[k]:
                yield due
                copy.wait_recv()
            whole[q][k].done = True

        to_sibling(0, x, pl.ds(0, slots))
        for where, far in ((low, 1), (high, -1)):
            region = lambda p, where=where: rows.at[p, c, where, cols]
            both_ways(
                lambda w, end, where=where, region=region, far=far: ring_gather(
                    ring_x, w, region, end, far,
                    lambda d, where=where: to_sibling(d % nx, lax.rem(x + nx - d, nx), where),
                )
            )

    def place_of(k):
        return lax.rem(x + nx - k, nx)

    def first_product(q):
        for k in [0] + [k for k in range(1, nx) if k != hops] + [hops]:
            yield whole[q][k]
            if q:
                yield multiplied[q - 1][k]
            yield Work(1.4)
            if q == 0 and k == 0:
                loads[0].wait()
            p = place_of(k)
            tile = min(256, ffw)

            @pl.loop(0, ffw // tile)
            def _(j):
                cols = pl.ds(pl.multiple_of(j * tile, tile), tile)
                value = dot(
                    rows[p, :, :, part_cols(q)].reshape(CORES * slots, wide), win[part_cols(q), cols]
                ).reshape(CORES, slots, tile)
                if q:
                    value = value + acc[p, :, :, cols]
                if q < n_part - 1:
                    acc[p, :, :, cols] = value
                else:
                    hid[p, :, :, cols] = jnp.maximum(value, 0.0).astype(BF16)

            multiplied[q][k].done = True
        hidden[q].done = True

    def second_product(q):
        yield hidden[n_part - 1]
        if q:
            yield Work(0.0, q)
        if q == 0:
            loads[2].wait()
        tile = min(256, wide)
        for j in range(wide // tile):
            yield Work(1.0, q)
            cols = pl.ds(q * wide + j * tile, tile)
            value = dot(hid[...].reshape(nx * CORES * slots, ffw), wout[:, cols])
            part[:, :, :, cols] = value.astype(BF16).reshape(nx, CORES, slots, tile)
        cols = part_cols(q)
        swaps = []
        for k in order:
            p = lax.rem(x + k, nx)
            swaps.append(send(part.at[p, 1 - c, :, cols], part_in.at[p, :, cols], sibling, "core"))
        for k, (copy, due) in zip(order, swaps):
            p = lax.rem(x + k, nx)
            yield due
            copy.wait_recv()
            add_into(part.at[p, c, :, cols], part_in.at[p, :, cols])
        ends = []
        for h, far in ((0, 1), (1, -1)):
            where = pl.ds(h * (slots // 2), slots // 2)
            own = lambda p, where=where: part.at[p, c, where, cols]
            landing = lambda w, where=where: lambda s: xr.at[q, (1 - w) // 2, s, where]
            ends += both_ways(
                lambda w, end, own=own, landing=landing, far=far: ring_sum(
                    ring_x, w, own, landing(w), end, far, 0.15
                )
            )
        for end in ends:
            yield end
        eout[:, cols] = part[x, c, :, cols]
        summed[q].done = True

    blocks = 2 if nz % 2 == 0 else 1
    step = blocks * ny * tok

    def student_forward():
        for event in gathered:
            yield event
        loads[1].wait()
        for k in range(group // step):
            yield Work(1.0, 5)
            at = k * step
            block = grp[k * blocks : (k + 1) * blocks, :, :, LANES : LANES + width].reshape(step, width)
            value = dot(block, up[...])
            sig = jax.nn.sigmoid(value)
            act = value * sig
            hstu[at : at + step, :] = act.astype(BF16)
            hT[:, at : at + step] = act.T.astype(BF16)
            sgT[:, at : at + step] = (sig * (1.0 + value * (1.0 - sig))).T
        student.done = True

    def combine(q):
        yield student
        yield summed[q]
        if q == 0:
            loads[3].wait()
        tile = min(512, wide)
        line = lax.broadcasted_iota(jnp.int32, (LANES, slots), 0)
        pick_rank = jnp.where(line == e, 1.0, 0.0).astype(BF16)
        pick_gate = jnp.where((line == e + 32) | (line == e + 64), 1.0, 0.0).astype(BF16)

        @pl.loop(0, group // step)
        def _(k):
            tab = grp[pl.ds(k * blocks, blocks), :, :, 0:LANES].reshape(step, LANES)
            ranks = dot(tab, pick_rank)
            gates = dot(tab, pick_gate)
            token = lax.broadcasted_iota(jnp.int32, (step, slots), 0) + k * step
            slot = lax.broadcasted_iota(jnp.int32, (step, slots), 1)
            chosen = (slot // CAP == token // tok) & (ranks == ((slot & (CAP - 1)) + 1).astype(F32))
            spread = jnp.where(chosen, 1.0, 0.0).astype(BF16)
            at = pl.multiple_of(k * step, step)
            for j in range(wide // tile):
                cols = slice(q * wide + j * tile, q * wide + (j + 1) * tile)
                value = dot(hstu[pl.ds(at, step), :], down[:, cols])
                value = value - gates[:, 0:1] * dot(spread, eout[:, cols])
                mix[pl.ds(k * blocks, blocks), :, :, cols] = value.astype(BF16).reshape(blocks, ny, tok, tile)

        plan.now += 1.7
        cols, end = columns(q, 0), Event()
        plan.spawn((sum_y_then_z if q == Z_FIRST else sum_z_then_y)(q, cols, end))
        yield end
        value = mix[z, y, :, cols].astype(F32)
        if q != Z_FIRST:
            for k in range(ny - 1):
                value = value + ys[k].astype(F32)
        og[z, y, :, cols] = (grp[z, y, :, 96:97].astype(F32) * scale * value).astype(BF16)
        plan.now += 0.3
        plan.spawn(gather_plane(og, q, 0, grads[q]))

    def to_places(kind):
        swap, due = send(gt.at[kind, :, 1 - c], gt_in.at[kind], sibling, "core")
        yield due
        swap.wait_recv()
        for p in range(nx):
            add_into(gt.at[kind, p, c], gt_in.at[kind, p])
        n = gt.shape[3]
        ends = []
        for h, far in ((0, 1), (1, -1)):
            where = pl.ds(h * (n // 2), n // 2)
            own = lambda p, where=where: gt.at[kind, p, c, where]
            landing = lambda w, where=where: lambda s: gr.at[kind, (1 - w) // 2, s, where]
            ends += both_ways(
                lambda w, end, own=own, landing=landing, far=far: ring_sum(
                    ring_x, w, own, landing(w), end, far, 0.05
                )
            )
        for end in ends:
            yield end
        if kind:
            gdown_ref[...] = gt[1, x, c].astype(F32)
        else:
            gup_ref[...] = gt[0, x, c].astype(F32).T

    def backward():
        per_part = nx * CORES // n_part
        for q in range(n_part):
            yield grads[q]
            yield Work(1.2)

            @pl.loop(0, per_part)
            def _(k):
                to = q * per_part + k
                cols = pl.ds(pl.multiple_of(to * share, share), share)
                value = dot(hT[...], og[:, :, :, cols].reshape(group, share))
                gt[1, to // CORES, lax.rem(to, CORES)] = value.astype(BF16)

            if q == n_part - 1:
                plan.spawn(to_places(1))
            yield Work(1.2)

            @pl.loop(0, group // step)
            def _(k):
                block = og[pl.ds(k * blocks, blocks), :, :, part_cols(q)].reshape(step, wide)
                place = pl.ds(pl.multiple_of(k * step, step), step)
                value = dot_nt(down[:, part_cols(q)], block)
                if q:
                    value = value + back[:, place]
                if q < n_part - 1:
                    back[:, place] = value
                else:
                    hgT[:, place] = (value * sgT[:, place]).astype(BF16)

        yield Work(2.2)

        @pl.loop(0, nx * CORES)
        def _(k):
            cols = pl.ds(pl.multiple_of(LANES + k * share, LANES), share)
            value = dot(hgT[...], grp[:, :, :, cols].reshape(group, share))
            gt[0, k // CORES, lax.rem(k, CORES)] = value.astype(BF16)

        plan.spawn(to_places(0))

    for q in range(n_part):
        plan.spawn(gather_plane(grp, q, LANES, gathered[q]))
        plan.spawn(take_slots(q))
        plan.spawn(first_product(q))
        plan.spawn(second_product(q))
        plan.spawn(combine(q))
    plan.spawn(student_forward())
    plan.spawn(backward())
    plan.run()

    for copy in sent:
        copy.wait_send()


def per_device(nz, ny, nx, tokens, expert_ids, gates, valid, w_in, w_out, up_proj, down_proj):
    tok, width = tokens.shape
    ffw, hidden = w_in.shape[2], up_proj.shape[1]
    group = nz * ny * tok
    slots = nz * ny * CAP
    share = width // (nx * CORES)
    scale = 1.0 / float(group * nx * CORES) ** 0.5
    n_part = 2
    wide = width // n_part
    copies = 320
    vmem = lambda shape, dtype=BF16: pltpu.VMEM(shape, dtype)
    scratch = [
        vmem((width, ffw)), vmem((ffw, width)), vmem((width, hidden)), vmem((hidden, width)),
        vmem((nz, ny, tok, width + LANES)),
        vmem((nx, CORES, slots, width)),
        vmem((nx, CORES, slots, ffw), F32),
        vmem((nx, CORES, slots, ffw)),
        vmem((nx, CORES, slots, width)),
        vmem((nx, slots, width)),
        vmem((n_part, 2, nx // 2, slots, wide)),
        vmem((slots, width)),
        vmem((group, hidden)),
        vmem((hidden, group)), vmem((hidden, group), F32), vmem((hidden, group)),
        vmem((hidden, group), F32),
        vmem((nz, ny, tok, width)),
        vmem((ny, 2, nz // 2, tok, wide)),
        vmem((nz, 2, ny // 2, tok, wide)),
        vmem((2, nz // 2, tok, wide)),
        vmem((ny - 1, tok, wide)),
        vmem((nz, ny, tok, width)),
        vmem((2, nx, CORES, hidden, share)),
        vmem((2, nx, hidden, share)),
        vmem((2, 2, nx // 2, hidden, share)),
        pltpu.SemaphoreType.DMA((copies,)),
        pltpu.SemaphoreType.DMA((copies,)),
        pltpu.SemaphoreType.DMA((4,)),
    ]
    in_vmem = pl.BlockSpec(memory_space=pltpu.VMEM)
    anywhere = pl.BlockSpec(memory_space=pl.ANY)
    return pl.pallas_call(
        functools.partial(kernel, nz, ny, nx, scale, n_part),
        out_shape=(
            jax.ShapeDtypeStruct((share, hidden), F32),
            jax.ShapeDtypeStruct((hidden, share), F32),
        ),
        in_specs=[in_vmem] * 4 + [anywhere] * 4,
        out_specs=(in_vmem, in_vmem),
        scratch_shapes=scratch,
        cost_estimate=pl.CostEstimate(flops=15 * 10**9, bytes_accessed=11 * 10**6, transcendentals=0),
        compiler_params=pltpu.CompilerParams(
            collective_id=0, has_side_effects=True, vmem_limit_bytes=61 * 2**20
        ),
    )(tokens, expert_ids.T, gates.T, valid.reshape(1, tok), w_in, w_out, up_proj, down_proj)


def solution(mesh):
    n_expert, n_dp = mesh.shape["expert"], mesh.shape["dp"]
    ny = 4 if n_expert >= 16 else 2
    nz, nx = n_expert // ny, n_dp // CORES
    return jax.shard_map(
        functools.partial(per_device, nz, ny, nx),
        mesh=mesh,
        in_specs=(
            P(("dp", "expert"), None),
            P(("dp", "expert"), None),
            P(("dp", "expert"), None),
            P(("dp", "expert")),
            P("expert", None, "dp"),
            P("expert", "dp", None),
            P(None, "expert"),
            P("expert", None),
        ),
        out_specs=(P("dp", "expert"), P("expert", "dp")),
        check_vma=False,
    )
```

time: 639 us -> 183 us (0.29)
  waiting for transfers between devices: 532 us -> 0 us
  Pallas kernels: 0 us -> 179 us
  matrix products: 35.9 us -> 0 us
  local copies, waits for them, and re-layouts: 28.9 us -> 3.34 us
  starting transfers between devices: 20 us -> 0 us
  between operations: 15.4 us -> 0.64 us
    reduce_scatter x4 -> x0, waiting for transfers between devices: 289 us -> none  [the longest x1 198 us: per_device(): lax.psum_scatter(partial_out.astype(jnp.bfloat16), 'expert', scatter_dime...]
    pallas_call x0 -> x1, Pallas kernels: none -> 179 us  [per_device(): pl.pallas_call(functools.partial(kernel, nz, ny, nx, scale, n_part), out_...]
    all_to_all x2 -> x0, waiting for transfers between devices: 121 us -> none  [the longest x1 109 us: per_device(): lax.all_to_all(stacked, 'expert', split_axis=1, concat_axis=2, tiled=True)]
    all_gather x3 -> x0, waiting for transfers between devices: 121 us -> none  [the longest x1 81.8 us: per_device(): group_grad = lax.all_gather(out_grad, 'expert', axis=0, tiled=True)]
    dot_general x8 -> x0, matrix products: 35.9 us -> none  [the longest x1 9.04 us: per_device(): lax.dot_general(group_tokens, hidden_grad, (((0,), (0,)), ((), ())), pref...]
    all_to_all x2 -> x0, starting transfers between devices: 19.4 us -> none  [the longest x1 9.7 us: per_device(): lax.all_to_all(stacked, 'expert', split_axis=1, concat_axis=2, tiled=True)]
    all_to_all x3 -> x0, local copies, waits for them, and re-layouts: 9.26 us -> none  [the longest x1 7.08 us: per_device(): lax.all_to_all(stacked, 'expert', split_axis=1, concat_axis=2, tiled=True)]
    reshape x3 -> x0, local copies, waits for them, and re-layouts: 8.25 us -> none  [the longest x1 6.96 us: per_device(): expert_rows = arrived.reshape(n_data * slot_width, tokens.shape[1])]
  transfers between devices with their start and end apart: 9 -> 0, of which waited for: 8 -> 0; matrix products, arithmetic and copies ran while one was open for 7% -> 0% of each run, Pallas kernels for 0% -> 0%
where the time goes in v3:
time: 183 us
  Pallas kernels  179 us (98%)
  local copies, waits for them, and re-layouts  3.34 us (2%)
    pallas_call x1, Pallas kernels, per_device(): pl.pallas_call(functools.partial(kernel, nz, ny, nx, scale, n_part), out_...  179 us

profile of v3, /device:TPU:1, one launch (start us, length us, event | category | flops | bytes accessed | tf_op | source)
XLA Modules:
  0.0 182.7 jit_solution(15084896599700813452)
XLA Ops:
  0.6 178.7 %shard_map.95 = (f32[256,256]{1,0:T(8,128)}, f32[256,256]{1,0:T(8,128)}) custom-call(bf16[32,2048]{1,0:T(8,128)(2,1)} %tok_ref.1, s32[2,32]{1,0:T(2,128)} %bitcast.3, f32[2,32]{1,0:T(2,128)} %bitcast.4, s32[1,32]{1,0:T(1,128)} %bitcast.5, bf16[1,2048,1024]{2,1,0:T(8,128)(2,1)} %win_hbm.1, bf16[1,1024,2048]{2,1,0:T(8,128)(2,1)} %wout_hbm.1, ...), custom_call_target="tpu_custom_call" | custom-call | flops 15000000512 | bytes 11000000 | tf_op jit(solution)/shard_map/pallas_call | solution.py:586
  179.4 1.7 copy.12
  181.0 1.7 copy.13

commit v4 on v3

--- a/solution.py
+++ b/solution.py
@@ -9,7 +9,10 @@
 
 MESH = pl.DeviceIdType.MESH
 CORES = 2
+SLACK = 3.0
 CAP = 4
+PLANE_HOPS = (("z1", 1.0), ("z-1", 1.0), ("y1", 0.5), ("y-1", 0.5))
+FOLD = 4
 LANES = 128
 Z_FIRST = 0
 F32, BF16 = jnp.float32, jnp.bfloat16
@@ -34,12 +37,14 @@
 
 
 class Plan:
-    RATE, INNER, LATENCY = 100e3, 400e3, 2.2
+    RATE, INNER, LATENCY = 100e3, 400e3, 4.0
 
     def __init__(self):
         self.now, self.busy, self.processes = 0.0, {}, []
 
     def transfer(self, link, nbytes):
+        if link == "plane":
+            return max(self.transfer(way, nbytes * hops) for way, hops in PLANE_HOPS) + self.LATENCY
         start = max(self.now, self.busy.get(link, 0.0))
         self.busy[link] = start + nbytes / (self.INNER if link == "core" else self.RATE / CORES)
         return self.busy[link] + self.LATENCY
@@ -81,8 +86,8 @@
 def kernel(
     nz, ny, nx, scale, n_part,
     tok_ref, ids_ref, gate_ref, valid_ref, win_hbm, wout_hbm, up_hbm, down_hbm,
-    gup_ref, gdown_ref,
-    win, wout, up, down, grp, rows, acc, hid, part, part_in, xr, eout,
+    grad_ref,
+    win, wout, up, down, grp, rows, acc, hid, part, part_in, xr, ret, got,
     hstu, hT, sgT, hgT, back, mix, zr, yr, zs, ys, og, gt, gt_in, gr,
     send_sem, recv_sem, load_sem,
 ):
@@ -117,8 +122,7 @@
 
     barrier = pltpu.get_barrier_semaphore()
     near = [sibling]
-    near += [at_z(k) for k in sorted({1, nz - 1})]
-    near += [at_y(k) for k in range(1, ny)]
+    near += [(lax.rem(e + k, nz * ny), g) for k in range(1, nz * ny)]
     near += [at_x(k) for k in sorted({1, nx - 1})]
     for device in near:
         pl.semaphore_signal(barrier, inc=1, device_id=device, device_id_type=MESH)
@@ -168,13 +172,13 @@
                 arrived(way * s)
         done.done = True
 
-    def ring_sum(ring, way, own, landing, done, far, us):
+    def ring_sum(ring, way, own, landing, done, far, us, slack=0.0):
         n, i, at, name = ring
         steps = n // 2 if way == far else n // 2 - 1
         for s in range(1, steps + 1):
             place = lax.rem(i + n + way * (steps - s + 1), n)
             copy, due = send(own(place), landing(s - 1), at(1 if way == 1 else n - 1), name + str(way))
-            yield due
+            yield due + slack
             copy.wait_recv()
             add_into(own(lax.rem(i + n + way * (steps - s), n)), landing(s - 1))
             plan.now += us
@@ -239,7 +243,7 @@
             own = lambda p: mix.at[p, to, :, cols]
             landing = lambda w: lambda s: zr.at[k, (1 - w) // 2, s]
             far = 1 if k in (0, 1) else -1
-            for end in both_ways(lambda w, end: ring_sum(ring_z, w, own, landing(w), end, far, 0.1)):
+            for end in both_ways(lambda w, end: ring_sum(ring_z, w, own, landing(w), end, far, 0.1, SLACK)):
                 yield end
             if k:
                 from_y.append(
@@ -264,7 +268,7 @@
             to = lax.rem(z + k, nz)
             own = lambda p: mix.at[to, p, :, cols]
             landing = lambda w: lambda s: yr.at[k, (1 - w) // 2, s]
-            for end in both_ways(lambda w, end: ring_sum(ring_y, w, own, landing(w), end, far, 0.1)):
+            for end in both_ways(lambda w, end: ring_sum(ring_y, w, own, landing(w), end, far, 0.1, SLACK)):
                 yield end
             finished[k].done = True
 
@@ -278,7 +282,7 @@
                     mix.at[lax.rem(i + n + way * k, n), y, :, cols], zs.at[(1 - way) // 2, s - 1],
                     at(1 if way == 1 else n - 1), name + str(way),
                 )
-                yield due
+                yield due + SLACK
                 copy.wait_recv()
                 yield finished[(way * (k - 1)) % n]
                 add_into(mix.at[lax.rem(i + n + way * (k - 1), n), y, :, cols], zs.at[(1 - way) // 2, s - 1])
@@ -407,7 +411,24 @@
             )
         for end in ends:
             yield end
-        eout[:, cols] = part[x, c, :, cols]
+        n_place, fold = nz * ny, wide // FOLD
+        i = lax.broadcasted_iota(jnp.int32, (n_place * CAP * FOLD, slots), 0)
+        slot = lax.broadcasted_iota(jnp.int32, (n_place * CAP * FOLD, slots), 1)
+        at_row = slot == (i >> 4) * CAP + (i & 3)
+        folded = jnp.zeros((n_place * CAP * FOLD, fold), F32)
+        for f in range(FOLD):
+            move = jnp.where(at_row & (((i >> 2) & 3) == f), 1.0, 0.0).astype(BF16)
+            folded = folded + dot(move, part[x, c, :, q * wide + f * fold : q * wide + (f + 1) * fold])
+        ret[q] = folded.astype(BF16).reshape(n_place, CAP * FOLD, fold)
+        got[q, e] = ret[q, e]
+        plan.now += 0.8
+        backs = []
+        for k in range(1, n_place):
+            to = lax.rem(e + k, n_place)
+            backs.append(send(ret.at[q, to], got.at[q, e], (to, g), "plane"))
+        for copy, due in backs:
+            yield due
+            copy.wait_recv()
         summed[q].done = True
 
     blocks = 2 if nz % 2 == 0 else 1
@@ -429,42 +450,50 @@
             sgT[:, at : at + step] = (sig * (1.0 + value * (1.0 - sig))).T
         student.done = True
 
-    def combine(q):
+    def student_output(q):
         yield student
-        yield summed[q]
+        yield Work(1.2, 6)
         if q == 0:
             loads[3].wait()
         tile = min(512, wide)
-        line = lax.broadcasted_iota(jnp.int32, (LANES, slots), 0)
-        pick_rank = jnp.where(line == e, 1.0, 0.0).astype(BF16)
-        pick_gate = jnp.where((line == e + 32) | (line == e + 64), 1.0, 0.0).astype(BF16)
 
         @pl.loop(0, group // step)
         def _(k):
-            tab = grp[pl.ds(k * blocks, blocks), :, :, 0:LANES].reshape(step, LANES)
-            ranks = dot(tab, pick_rank)
-            gates = dot(tab, pick_gate)
-            token = lax.broadcasted_iota(jnp.int32, (step, slots), 0) + k * step
-            slot = lax.broadcasted_iota(jnp.int32, (step, slots), 1)
-            chosen = (slot // CAP == token // tok) & (ranks == ((slot & (CAP - 1)) + 1).astype(F32))
-            spread = jnp.where(chosen, 1.0, 0.0).astype(BF16)
             at = pl.multiple_of(k * step, step)
             for j in range(wide // tile):
                 cols = slice(q * wide + j * tile, q * wide + (j + 1) * tile)
                 value = dot(hstu[pl.ds(at, step), :], down[:, cols])
-                value = value - gates[:, 0:1] * dot(spread, eout[:, cols])
                 mix[pl.ds(k * blocks, blocks), :, :, cols] = value.astype(BF16).reshape(blocks, ny, tok, tile)
 
-        plan.now += 1.7
-        cols, end = columns(q, 0), Event()
-        plan.spawn((sum_y_then_z if q == Z_FIRST else sum_z_then_y)(q, cols, end))
-        yield end
+        plan.spawn((sum_y_then_z if q == Z_FIRST else sum_z_then_y)(q, columns(q, 0), mixed[q]))
+
+    def output_grad(q):
+        yield mixed[q]
+        yield summed[q]
+        cols = columns(q, 0)
         value = mix[z, y, :, cols].astype(F32)
         if q != Z_FIRST:
             for k in range(ny - 1):
                 value = value + ys[k].astype(F32)
+        n_row = nz * ny * CAP * FOLD
+        table = grp[z, y, :, 0:LANES]
+        line = lax.broadcasted_iota(jnp.int32, (LANES, n_row), 0)
+        source = lax.broadcasted_iota(jnp.int32, (LANES, n_row), 1) >> 4
+        spread = lambda off: dot(table, jnp.where(line == source + off, 1.0, 0.0).astype(BF16))
+        ranks, high, low = spread(0), spread(32), spread(64)
+        i = lax.broadcasted_iota(jnp.int32, (tok, n_row), 1)
+        named = ranks == ((i & 3) + 1).astype(F32)
+        back_rows = got[q].reshape(n_row, wide // FOLD)
+        pieces = []
+        for f in range(FOLD):
+            here = named & (((i >> 2) & 3) == f)
+            pieces.append(
+                dot(jnp.where(here, high, 0.0).astype(BF16), back_rows)
+                + dot(jnp.where(here, low, 0.0).astype(BF16), back_rows)
+            )
+        value = value - jnp.concatenate(pieces, axis=1)
         og[z, y, :, cols] = (grp[z, y, :, 96:97].astype(F32) * scale * value).astype(BF16)
-        plan.now += 0.3
+        plan.now += 0.8
         plan.spawn(gather_plane(og, q, 0, grads[q]))
 
     def to_places(kind):
@@ -487,9 +516,9 @@
         for end in ends:
             yield end
         if kind:
-            gdown_ref[...] = gt[1, x, c].astype(F32)
+            grad_ref[1] = gt[1, x, c]
         else:
-            gup_ref[...] = gt[0, x, c].astype(F32).T
+            grad_ref[0] = gt[0, x, c].astype(F32).T.astype(BF16)
 
     def backward():
         per_part = nx * CORES // n_part
@@ -535,7 +564,8 @@
         plan.spawn(take_slots(q))
         plan.spawn(first_product(q))
         plan.spawn(second_product(q))
-        plan.spawn(combine(q))
+        plan.spawn(student_output(q))
+        plan.spawn(output_grad(q))
     plan.spawn(student_forward())
     plan.spawn(backward())
     plan.run()
@@ -553,7 +583,7 @@
     scale = 1.0 / float(group * nx * CORES) ** 0.5
     n_part = 2
     wide = width // n_part
-    copies = 320
+    copies = 384
     vmem = lambda shape, dtype=BF16: pltpu.VMEM(shape, dtype)
     scratch = [
         vmem((width, ffw)), vmem((ffw, width)), vmem((width, hidden)), vmem((hidden, width)),
@@ -564,7 +594,8 @@
         vmem((nx, CORES, slots, width)),
         vmem((nx, slots, width)),
         vmem((n_part, 2, nx // 2, slots, wide)),
-        vmem((slots, width)),
+        vmem((n_part, nz * ny, CAP * FOLD, wide // FOLD)),
+        vmem((n_part, nz * ny, CAP * FOLD, wide // FOLD)),
         vmem((group, hidden)),
         vmem((hidden, group)), vmem((hidden, group), F32), vmem((hidden, group)),
         vmem((hidden, group), F32),
@@ -583,20 +614,18 @@
     ]
     in_vmem = pl.BlockSpec(memory_space=pltpu.VMEM)
     anywhere = pl.BlockSpec(memory_space=pl.ANY)
-    return pl.pallas_call(
+    grads = pl.pallas_call(
         functools.partial(kernel, nz, ny, nx, scale, n_part),
-        out_shape=(
-            jax.ShapeDtypeStruct((share, hidden), F32),
-            jax.ShapeDtypeStruct((hidden, share), F32),
-        ),
+        out_shape=jax.ShapeDtypeStruct((2, share, hidden), BF16),
         in_specs=[in_vmem] * 4 + [anywhere] * 4,
-        out_specs=(in_vmem, in_vmem),
+        out_specs=in_vmem,
         scratch_shapes=scratch,
         cost_estimate=pl.CostEstimate(flops=15 * 10**9, bytes_accessed=11 * 10**6, transcendentals=0),
         compiler_params=pltpu.CompilerParams(
             collective_id=0, has_side_effects=True, vmem_limit_bytes=61 * 2**20
         ),
     )(tokens, expert_ids.T, gates.T, valid.reshape(1, tok), w_in, w_out, up_proj, down_proj)
+    return grads[0].astype(F32), grads[1].reshape(hidden, share).astype(F32)
 
 
 def solution(mesh):

time: 183 us -> 163 us (0.89)
  Pallas kernels: 179 us -> 160 us
  local copies, waits for them, and re-layouts: 3.34 us -> 0 us
    pallas_call x1, Pallas kernels: 179 us -> 160 us  [per_device(): pl.pallas_call(functools.partial(kernel, nz, ny, nx, scale, n_part), out_...]
    unnamed x2 -> x0, local copies, waits for them, and re-layouts: 3.34 us -> none
where the time goes in v4:
time: 163 us
  Pallas kernels  160 us (98%)
  other arithmetic  1.79 us (1%)
    pallas_call x1, Pallas kernels, per_device(): pl.pallas_call(functools.partial(kernel, nz, ny, nx, scale, n_part), out_...  160 us

profile of v4, /device:TPU:1, one launch (start us, length us, event | category | flops | bytes accessed | tf_op | source)
XLA Modules:
  0.0 162.9 jit_solution(97565750196698534)
XLA Ops:
  0.6 160.5 %shard_map.95 = bf16[2,256,256]{2,1,0:T(8,128)(2,1)} custom-call(bf16[32,2048]{1,0:T(8,128)(2,1)} %tok_ref.1, s32[2,32]{1,0:T(2,128)} %bitcast.9, f32[2,32]{1,0:T(2,128)} %bitcast.10, s32[1,32]{1,0:T(1,128)} %bitcast.11, bf16[1,2048,1024]{2,1,0:T(8,128)(2,1)} %win_hbm.1, bf16[1,1024,2048]{2,1,0:T(8,128)(2,1)} %wout_hbm.1, bf16[2048,256]{1,0:T(8,128)(2,1)} %up_hbm.1, ...), custom_call_target="tpu_custom_call" | custom-call | flops 15000000512 | bytes 11000000 | tf_op jit(solution)/shard_map/pallas_call | solution.py:617
  161.1 1.8 %bitcast_convert_fusion = (f32[256,256]{1,0:T(8,128)}, f32[256,256]{1,0:T(8,128)}) fusion(bf16[2,256,256]{2,1,0:T(8,128)(2,1)} %shard_map.95), kind=kLoop, calls=%fused_computation | loop fusion | flops 131072 | bytes 786432 | tf_op jit(solution)/shard_map/convert_element_type | solution.py:628

commit v5 on v4

--- a/solution.py
+++ b/solution.py
@@ -9,7 +9,7 @@
 
 MESH = pl.DeviceIdType.MESH
 CORES = 2
-SLACK = 3.0
+SLACK = 6.0
 CAP = 4
 PLANE_HOPS = (("z1", 1.0), ("z-1", 1.0), ("y1", 0.5), ("y-1", 0.5))
 FOLD = 4

time: 163 us -> 168 us (1.031)
  Pallas kernels: 160 us -> 166 us
    pallas_call x1, Pallas kernels: 160 us -> 166 us  [per_device(): pl.pallas_call(functools.partial(kernel, nz, ny, nx, scale, n_part), out_...]
where the time goes in v5:
time: 168 us
  Pallas kernels  166 us (99%)
  other arithmetic  1.79 us (1%)
    pallas_call x1, Pallas kernels, per_device(): pl.pallas_call(functools.partial(kernel, nz, ny, nx, scale, n_part), out_...  166 us

profile of v5, /device:TPU:1, one launch (start us, length us, event | category | flops | bytes accessed | tf_op | source)
XLA Modules:
  0.0 168.0 jit_solution(1645465082980703894)
XLA Ops:
  0.6 165.6 %shard_map.95 = bf16[2,256,256]{2,1,0:T(8,128)(2,1)} custom-call(bf16[32,2048]{1,0:T(8,128)(2,1)} %tok_ref.1, s32[2,32]{1,0:T(2,128)} %bitcast.9, f32[2,32]{1,0:T(2,128)} %bitcast.10, s32[1,32]{1,0:T(1,128)} %bitcast.11, bf16[1,2048,1024]{2,1,0:T(8,128)(2,1)} %win_hbm.1, bf16[1,1024,2048]{2,1,0:T(8,128)(2,1)} %wout_hbm.1, bf16[2048,256]{1,0:T(8,128)(2,1)} %up_hbm.1, ...), custom_call_target="tpu_custom_call" | custom-call | flops 15000000512 | bytes 11000000 | tf_op jit(solution)/shard_map/pallas_call | solution.py:617
  166.2 1.8 %bitcast_convert_fusion = (f32[256,256]{1,0:T(8,128)}, f32[256,256]{1,0:T(8,128)}) fusion(bf16[2,256,256]{2,1,0:T(8,128)(2,1)} %shard_map.95), kind=kLoop, calls=%fused_computation | loop fusion | flops 131072 | bytes 786432 | tf_op jit(solution)/shard_map/convert_element_type | solution.py:628

commit v6 on v4

--- a/solution.py
+++ b/solution.py
@@ -37,7 +37,7 @@
 
 
 class Plan:
-    RATE, INNER, LATENCY = 100e3, 400e3, 4.0
+    RATE, INNER, LATENCY = 100e3, 400e3, 5.0
 
     def __init__(self):
         self.now, self.busy, self.processes = 0.0, {}, []

time: 163 us -> 165 us (1.012)
  Pallas kernels: 160 us -> 163 us
    pallas_call x1, Pallas kernels: 160 us -> 163 us  [per_device(): pl.pallas_call(functools.partial(kernel, nz, ny, nx, scale, n_part), out_...]
where the time goes in v6:
time: 165 us
  Pallas kernels  163 us (99%)
  other arithmetic  1.79 us (1%)
    pallas_call x1, Pallas kernels, per_device(): pl.pallas_call(functools.partial(kernel, nz, ny, nx, scale, n_part), out_...  163 us

profile of v6, /device:TPU:1, one launch (start us, length us, event | category | flops | bytes accessed | tf_op | source)
XLA Modules:
  0.0 165.0 jit_solution(6978226222694923550)
XLA Ops:
  0.6 162.6 %shard_map.95 = bf16[2,256,256]{2,1,0:T(8,128)(2,1)} custom-call(bf16[32,2048]{1,0:T(8,128)(2,1)} %tok_ref.1, s32[2,32]{1,0:T(2,128)} %bitcast.9, f32[2,32]{1,0:T(2,128)} %bitcast.10, s32[1,32]{1,0:T(1,128)} %bitcast.11, bf16[1,2048,1024]{2,1,0:T(8,128)(2,1)} %win_hbm.1, bf16[1,1024,2048]{2,1,0:T(8,128)(2,1)} %wout_hbm.1, bf16[2048,256]{1,0:T(8,128)(2,1)} %up_hbm.1, ...), custom_call_target="tpu_custom_call" | custom-call | flops 15000000512 | bytes 11000000 | tf_op jit(solution)/shard_map/pallas_call | solution.py:617
  163.2 1.8 %bitcast_convert_fusion = (f32[256,256]{1,0:T(8,128)}, f32[256,256]{1,0:T(8,128)}) fusion(bf16[2,256,256]{2,1,0:T(8,128)(2,1)} %shard_map.95), kind=kLoop, calls=%fused_computation | loop fusion | flops 131072 | bytes 786432 | tf_op jit(solution)/shard_map/convert_element_type | solution.py:628
